TPU v7x, 256 devices: a whole 4x4x8 slice. The times are simulated.
256 devices in a mesh: seq: 32 (over x, y, core), kv: 8 (over z).
Axes of the slice: x: 4, y: 4, z: 8, core: 2. Of those that a mesh axis runs over, the one named last changes fastest.
Arguments:
- query_rows: bfloat16 [8192, 8192], P(('seq', 'kv')), may hold values from -6 to 6
- attn_out: bfloat16 [8192, 8192], P(('seq', 'kv')), may hold values from -3 to 3
- grad_out: bfloat16 [8192, 8192], P(('seq', 'kv')), may hold values from -48 to 48
- logsumexp: float32 [64, 8192], P('kv', 'seq'), may hold values from 2.5 to 10.5
- key_cache: bfloat16 [8, 16384, 128], P('kv', 'seq'), may hold values from -6 to 6
- value_cache: bfloat16 [8, 16384, 128], P('kv', 'seq'), may hold values from -6 to 6
- block_lists: int32 [64, 64, 32], P('kv', 'seq'), may hold values from 0 to 127, as said below
- block_counts: int32 [64, 64], P('kv', 'seq'), may hold values from 2 to 32
Outputs:
- grad_query: bfloat16 [8192, 8192], P(('seq', 'kv'))
- grad_key: bfloat16 [8, 16384, 128], P('kv', 'seq')
- grad_value: bfloat16 [8, 16384, 128], P('kv', 'seq')
Inputs may be any that keep to these rules, and one draw needn't show every extreme that they name: `block_lists`: for head h and query block q (context block 64 + q), entries 0 to block_counts[h, q] - 1 are distinct KV blocks, none after the query block's own block, entry 0 being that own block; later entries are 0. Over the heads of one KV group and the query blocks of one seq index, the lists name at most 2 distinct blocks among the 4 blocks of any one seq index, and in every draw there is a seq index whose blocks are named exactly 2 distinct times by every group at every seq index.
All inputs are finite; a program needn't handle non-finite values.
Results may differ from a plain program's by a relative error of at most 0.018.
Values may be sent and summed in bfloat16 or wider, within the bound.
A program may use at most 64 MiB of HBM per device.

v0:
```python
import math

import jax
import jax.numpy as jnp
from jax import lax
from jax.sharding import PartitionSpec as P

BLK = 128


def on_device(
    query_rows, attn_out, grad_out, logsumexp, key_cache, value_cache, block_lists, block_counts
):
    groups = key_cache.shape[0]
    cache_len = key_cache.shape[1]
    head_dim = key_cache.shape[2]
    local_heads = block_lists.shape[0]
    per_group = local_heads // groups
    qblocks = block_lists.shape[1]
    list_len = block_lists.shape[2]
    owners = lax.axis_size("seq")
    seq_index = lax.axis_index("seq")
    cache_blocks = cache_len // BLK
    total_blocks = owners * cache_blocks
    slot_count = owners * qblocks
    window = qblocks * BLK
    score_scale = 1.0 / math.sqrt(head_dim)
    gathered_q, gathered_out, gathered_grad = (
        lax.all_to_all(query_rows, "kv", split_axis=1, concat_axis=0, tiled=True),
        lax.all_to_all(attn_out, "kv", split_axis=1, concat_axis=0, tiled=True),
        lax.all_to_all(grad_out, "kv", split_axis=1, concat_axis=0, tiled=True),
    )
    products = gathered_grad.astype(jnp.float32) * gathered_out.astype(jnp.float32)
    row_terms = jnp.sum(products.reshape(window, local_heads, head_dim), axis=2).T
    query_five = gathered_q.reshape(qblocks, BLK, groups, per_group, head_dim)
    grad_five = gathered_grad.reshape(qblocks, BLK, groups, per_group, head_dim)
    row_delta = row_terms.reshape(groups, per_group, qblocks, BLK)
    row_lse = logsumexp.reshape(groups, per_group, qblocks, BLK)
    list_rows = block_lists.reshape(groups, per_group, qblocks, list_len)
    count_rows = block_counts.reshape(groups, per_group, qblocks)
    live_slots = jnp.arange(list_len) < count_rows[..., None]
    block_ids = jnp.arange(total_blocks)
    named_blocks = jnp.any(
        (list_rows[..., None] == block_ids) & live_slots[..., None], axis=(1, 2, 3)
    )
    named_owner = named_blocks.reshape(groups, owners, cache_blocks).astype(jnp.int32)
    owner_rank = jnp.cumsum(named_owner, axis=2) - named_owner
    chosen = (named_owner[..., None] == 1) & (owner_rank[..., None] == jnp.arange(qblocks))
    requests = jnp.sum(jnp.where(chosen, jnp.arange(cache_blocks)[:, None], 0), axis=2)
    slot_of = (jnp.arange(owners)[:, None] * qblocks + owner_rank).reshape(groups, total_blocks)
    requested = lax.all_to_all(requests, "seq", split_axis=1, concat_axis=1, tiled=True)
    group_base = jnp.arange(groups)[:, None, None]
    paired = jnp.concatenate([key_cache, value_cache], axis=2).reshape(
        groups * cache_blocks, BLK, 2 * head_dim
    )
    served = paired[(requested + group_base * cache_blocks).reshape(-1)]
    served = served.reshape(groups, owners, qblocks, BLK, 2 * head_dim)
    fetched = lax.all_to_all(served, "seq", split_axis=1, concat_axis=1, tiled=True).reshape(
        groups * slot_count, BLK, 2 * head_dim
    )
    slot_index = jnp.take_along_axis(slot_of, list_rows.reshape(groups, -1), axis=1).reshape(
        list_rows.shape
    )
    slot_index = (
        jnp.where(live_slots, slot_index, 0) + jnp.arange(groups)[:, None, None, None] * slot_count
    )
    step_width = 4
    own_block = owners * qblocks + seq_index * qblocks + jnp.arange(qblocks)
    causal = jnp.arange(BLK)[None, :] <= jnp.arange(BLK)[:, None]

    def one_round(turn_index, carry):
        grad_q, grad_k, grad_v = carry
        begin_at = turn_index * step_width
        slot_rows = lax.dynamic_slice_in_dim(slot_index, begin_at, step_width, axis=3)
        alive_now = lax.dynamic_slice_in_dim(live_slots, begin_at, step_width, axis=3)
        picked = lax.dynamic_slice_in_dim(list_rows, begin_at, step_width, axis=3)
        tile_pairs = fetched[slot_rows]
        tile_keys = tile_pairs[..., :head_dim]
        tile_values = tile_pairs[..., head_dim:]
        scores = (
            jnp.einsum(
                "qtghd,ghqjsd->ghqjts", query_five, tile_keys, preferred_element_type=jnp.float32
            )
            * score_scale
        )
        diagonal = picked == own_block[None, None, :, None]
        allowed = alive_now[..., None, None] & (jnp.logical_not(diagonal)[..., None, None] | causal)
        weights = jnp.where(allowed, jnp.exp(scores - row_lse[:, :, :, None, :, None]), 0.0)
        grad_weights = jnp.einsum(
            "qtghd,ghqjsd->ghqjts", grad_five, tile_values, preferred_element_type=jnp.float32
        )
        grad_scores = weights * (grad_weights - row_delta[:, :, :, None, :, None])
        weights_half = weights.astype(jnp.bfloat16)
        scores_half = grad_scores.astype(jnp.bfloat16)
        grad_q = grad_q + jnp.einsum(
            "ghqjts,ghqjsd->qtghd", scores_half, tile_keys, preferred_element_type=jnp.float32
        )
        key_terms = jnp.einsum(
            "ghqjts,qtghd->ghqjsd", scores_half, query_five, preferred_element_type=jnp.float32
        )
        value_terms = jnp.einsum(
            "ghqjts,qtghd->ghqjsd", weights_half, grad_five, preferred_element_type=jnp.float32
        )
        flat_slots = slot_rows.reshape(-1)
        grad_k = grad_k.at[flat_slots].add(key_terms.reshape(-1, BLK, head_dim))
        grad_v = grad_v.at[flat_slots].add(value_terms.reshape(-1, BLK, head_dim))
        return (grad_q, grad_k, grad_v)

    rounds = (jnp.max(block_counts) + step_width - 1) // step_width
    initial = (
        jnp.zeros(query_five.shape, jnp.float32),
        jnp.zeros((groups * slot_count, BLK, head_dim), jnp.float32),
        jnp.zeros((groups * slot_count, BLK, head_dim), jnp.float32),
    )
    grad_q, grad_k, grad_v = lax.fori_loop(0, rounds, one_round, initial)
    query_grad = (grad_q * score_scale).astype(jnp.bfloat16).reshape(window, local_heads * head_dim)
    grad_query = lax.all_to_all(query_grad, "kv", split_axis=0, concat_axis=1, tiled=True)
    block_of = (jnp.arange(owners)[:, None] * cache_blocks + requests).reshape(groups, slot_count)
    slot_pairs = jnp.concatenate(
        [
            grad_k.reshape(groups, slot_count, BLK, head_dim),
            grad_v.reshape(groups, slot_count, BLK, head_dim),
        ],
        axis=3,
    )
    selector = (block_of[..., None] == jnp.arange(lax.axis_size("seq") * cache_blocks)).astype(
        jnp.float32
    )
    owned = lax.psum_scatter(
        jnp.einsum(
            "gcb,gcsd->bgsd",
            selector,
            slot_pairs,
            precision=lax.Precision.HIGHEST,
            preferred_element_type=jnp.float32,
        ).astype(jnp.bfloat16),
        "seq",
        scatter_dimension=0,
        tiled=True,
    ).astype(jnp.float32)
    owned_keys = jnp.transpose(owned[..., :head_dim], (1, 0, 2, 3))
    owned_values = jnp.transpose(owned[..., head_dim:], (1, 0, 2, 3))
    grad_key = (owned_keys * score_scale).astype(jnp.bfloat16).reshape(groups, cache_len, head_dim)
    grad_value = owned_values.astype(jnp.bfloat16).reshape(groups, cache_len, head_dim)
    return (grad_query, grad_key, grad_value)


def solution(mesh):
    placed = (
        P(("seq", "kv"), None),
        P(("seq", "kv"), None),
        P(("seq", "kv"), None),
        P("kv", "seq"),
        P("kv", "seq", None),
        P("kv", "seq", None),
        P("kv", "seq", None),
        P("kv", "seq"),
    )
    return jax.shard_map(
        on_device,
        mesh=mesh,
        in_specs=placed,
        out_specs=(P(("seq", "kv"), None), P("kv", "seq", None), P("kv", "seq", None)),
        check_vma=False,
    )
```

profile of v0, /device:TPU:1, one launch (start us, length us, event | category | flops | bytes accessed | tf_op | source)
XLA Modules:
  0.0 676.4 jit_solution(14276966717237988743)
XLA Ops:
  10.4 8.6 %all-to-all-start = ((s32[1,32,2]{2,0,1:T(1,128)}), s32[1,32,2]{2,0,1:T(1,128)S(1)}, u32[]{:S(2)}, u32[]{:S(2)}) async-start(s32[1,32,2]{2,0,1:T(1,128)} %copy.132), calls=%async_computation | async-start | bytes 32768 | tf_op jit(solution)/shard_map/all_to_all | solution.py:51
  20.9 5.0 all-to-all-done
  25.9 8.2 %all-to-all-start.2 = ((bf16[32,8,1024]{2,0,1:T(8,128)(2,1)}), bf16[32,8,1024]{2,0,1:T(8,128)(2,1)S(1)}, u32[]{:S(2)}, u32[]{:S(2)}) async-start(bf16[32,8,1024]{2,0,1:T(8,128)(2,1)} %bitcast.173), calls=%async_computation.2 | async-start | bytes 1048576 | tf_op jit(solution)/shard_map/all_to_all | solution.py:29
  35.9 16.1 %all-to-all-done.2 = bf16[32,8,1024]{2,0,1:T(8,128)(2,1)S(1)} async-done(((bf16[32,8,1024]{2,0,1:T(8,128)(2,1)}), bf16[32,8,1024]{2,0,1:T(8,128)(2,1)S(1)}, u32[]{:S(2)}, u32[]{:S(2)}) %all-to-all-start.2) | async-done | bytes 524320 | tf_op jit(solution)/shard_map/all_to_all | solution.py:29
  56.4 17.0 %all-to-all-done.4 = bf16[32,8,1024]{2,0,1:T(8,128)(2,1)S(1)} async-done(((bf16[32,8,1024]{2,0,1:T(8,128)(2,1)}), bf16[32,8,1024]{2,0,1:T(8,128)(2,1)S(1)}, u32[]{:S(2)}, u32[]{:S(2)}) %all-to-all-start.4) | async-done | bytes 524320 | tf_op jit(solution)/shard_map/all_to_all | solution.py:30
  81.1 13.7 %all-to-all-done.3 = bf16[32,8,1024]{2,0,1:T(8,128)(2,1)S(1)} async-done(((bf16[32,8,1024]{2,0,1:T(8,128)(2,1)}), bf16[32,8,1024]{2,0,1:T(8,128)(2,1)S(1)}, u32[]{:S(2)}, u32[]{:S(2)}) %all-to-all-start.3) | async-done | bytes 524320 | tf_op jit(solution)/shard_map/all_to_all | solution.py:31
  94.8 5.1 all-to-all-start.1
  109.2 43.0 %all-to-all-done.1 = bf16[1,32,2,128,256]{4,3,2,0,1:T(8,128)(2,1)} async-done(((bf16[1,32,2,128,256]{4,3,2,0,1:T(8,128)(2,1)}), bf16[1,32,2,128,256]{4,3,2,0,1:T(8,128)(2,1)}, u32[]{:S(2)}, u32[]{:S(2)}) %all-to-all-start.1) | async-done | bytes 4194336 | tf_op jit(solution)/shard_map/all_to_all | solution.py:58
  158.2 376.1 %while.15 = (s32[]{:T(128)}, f32[2,128,1,8,128]{1,4,3,0,2:T(8,128)}, f32[64,128,128]{2,1,0:T(8,128)}, f32[64,128,128]{2,1,0:T(8,128)}, s32[]{:T(128)}, /*index=5...) while((s32[]{:T(128)}, ...), condition=%wide.region_8.9_spmd.clone, body=%wide.region_5.8_spmd.clone.sunk | while | flops 1359234560 | bytes 96592264 | solution.py:115
  172.7 13.4 %scatter_fusion.1 = f32[64,128,128]{2,1,0:T(8,128)} fusion(f32[64,128,128]{2,1,0:T(8,128)} %get-tuple-element.338, s32[64]{0:T(128)S(1)} %fusion.82, f32[64,128,128]{2,1,0:T(8,128)} %bitcast.222), kind=kCustom, calls=%fused_computation.4.clone.clone.1 | custom fusion | flops 1048576 | bytes 12583168 | tf_op jit(solution)/shard_map/while/body/scatter-add | solution.py:106
  188.8 13.4 %scatter_fusion = f32[64,128,128]{2,1,0:T(8,128)} fusion(f32[64,128,128]{2,1,0:T(8,128)} %get-tuple-element.337, s32[64]{0:T(128)S(1)} %fusion.82, f32[64,128,128]{2,1,0:T(8,128)} %bitcast.223), kind=kCustom, calls=%fused_computation.3.clone.clone.1 | custom fusion | flops 1048576 | bytes 12583168 | tf_op jit(solution)/shard_map/while/body/scatter-add | solution.py:105
  202.8 5.0 gather_fusion
  216.7 14.4 %scatter_fusion.1 = f32[64,128,128]{2,1,0:T(8,128)} fusion(f32[64,128,128]{2,1,0:T(8,128)} %get-tuple-element.338, s32[64]{0:T(128)S(1)} %fusion.82, f32[64,128,128]{2,1,0:T(8,128)} %bitcast.222), kind=kCustom, calls=%fused_computation.4.clone.clone.1 | custom fusion | flops 1048576 | bytes 12583168 | tf_op jit(solution)/shard_map/while/body/scatter-add | solution.py:106
  233.7 13.6 %scatter_fusion = f32[64,128,128]{2,1,0:T(8,128)} fusion(f32[64,128,128]{2,1,0:T(8,128)} %get-tuple-element.337, s32[64]{0:T(128)S(1)} %fusion.82, f32[64,128,128]{2,1,0:T(8,128)} %bitcast.223), kind=kCustom, calls=%fused_computation.3.clone.clone.1 | custom fusion | flops 1048576 | bytes 12583168 | tf_op jit(solution)/shard_map/while/body/scatter-add | solution.py:105
  247.9 5.0 gather_fusion
  261.8 15.7 %scatter_fusion.1 = f32[64,128,128]{2,1,0:T(8,128)} fusion(f32[64,128,128]{2,1,0:T(8,128)} %get-tuple-element.338, s32[64]{0:T(128)S(1)} %fusion.82, f32[64,128,128]{2,1,0:T(8,128)} %bitcast.222), kind=kCustom, calls=%fused_computation.4.clone.clone.1 | custom fusion | flops 1048576 | bytes 12583168 | tf_op jit(solution)/shard_map/while/body/scatter-add | solution.py:106
  280.1 14.2 %scatter_fusion = f32[64,128,128]{2,1,0:T(8,128)} fusion(f32[64,128,128]{2,1,0:T(8,128)} %get-tuple-element.337, s32[64]{0:T(128)S(1)} %fusion.82, f32[64,128,128]{2,1,0:T(8,128)} %bitcast.223), kind=kCustom, calls=%fused_computation.3.clone.clone.1 | custom fusion | flops 1048576 | bytes 12583168 | tf_op jit(solution)/shard_map/while/body/scatter-add | solution.py:105
  308.8 16.1 %scatter_fusion.1 = f32[64,128,128]{2,1,0:T(8,128)} fusion(f32[64,128,128]{2,1,0:T(8,128)} %get-tuple-element.338, s32[64]{0:T(128)S(1)} %fusion.82, f32[64,128,128]{2,1,0:T(8,128)} %bitcast.222), kind=kCustom, calls=%fused_computation.4.clone.clone.1 | custom fusion | flops 1048576 | bytes 12583168 | tf_op jit(solution)/shard_map/while/body/scatter-add | solution.py:106
  327.5 14.3 %scatter_fusion = f32[64,128,128]{2,1,0:T(8,128)} fusion(f32[64,128,128]{2,1,0:T(8,128)} %get-tuple-element.337, s32[64]{0:T(128)S(1)} %fusion.82, f32[64,128,128]{2,1,0:T(8,128)} %bitcast.223), kind=kCustom, calls=%fused_computation.3.clone.clone.1 | custom fusion | flops 1048576 | bytes 12583168 | tf_op jit(solution)/shard_map/while/body/scatter-add | solution.py:105
  356.3 16.5 %scatter_fusion.1 = f32[64,128,128]{2,1,0:T(8,128)} fusion(f32[64,128,128]{2,1,0:T(8,128)} %get-tuple-element.338, s32[64]{0:T(128)S(1)} %fusion.82, f32[64,128,128]{2,1,0:T(8,128)} %bitcast.222), kind=kCustom, calls=%fused_computation.4.clone.clone.1 | custom fusion | flops 1048576 | bytes 12583168 | tf_op jit(solution)/shard_map/while/body/scatter-add | solution.py:106
  375.5 14.5 %scatter_fusion = f32[64,128,128]{2,1,0:T(8,128)} fusion(f32[64,128,128]{2,1,0:T(8,128)} %get-tuple-element.337, s32[64]{0:T(128)S(1)} %fusion.82, f32[64,128,128]{2,1,0:T(8,128)} %bitcast.223), kind=kCustom, calls=%fused_computation.3.clone.clone.1 | custom fusion | flops 1048576 | bytes 12583168 | tf_op jit(solution)/shard_map/while/body/scatter-add | solution.py:105
  404.5 16.4 %scatter_fusion.1 = f32[64,128,128]{2,1,0:T(8,128)} fusion(f32[64,128,128]{2,1,0:T(8,128)} %get-tuple-element.338, s32[64]{0:T(128)S(1)} %fusion.82, f32[64,128,128]{2,1,0:T(8,128)} %bitcast.222), kind=kCustom, calls=%fused_computation.4.clone.clone.1 | custom fusion | flops 1048576 | bytes 12583168 | tf_op jit(solution)/shard_map/while/body/scatter-add | solution.py:106
  423.5 14.5 %scatter_fusion = f32[64,128,128]{2,1,0:T(8,128)} fusion(f32[64,128,128]{2,1,0:T(8,128)} %get-tuple-element.337, s32[64]{0:T(128)S(1)} %fusion.82, f32[64,128,128]{2,1,0:T(8,128)} %bitcast.223), kind=kCustom, calls=%fused_computation.3.clone.clone.1 | custom fusion | flops 1048576 | bytes 12583168 | tf_op jit(solution)/shard_map/while/body/scatter-add | solution.py:105
  452.5 16.4 %scatter_fusion.1 = f32[64,128,128]{2,1,0:T(8,128)} fusion(f32[64,128,128]{2,1,0:T(8,128)} %get-tuple-element.338, s32[64]{0:T(128)S(1)} %fusion.82, f32[64,128,128]{2,1,0:T(8,128)} %bitcast.222), kind=kCustom, calls=%fused_computation.4.clone.clone.1 | custom fusion | flops 1048576 | bytes 12583168 | tf_op jit(solution)/shard_map/while/body/scatter-add | solution.py:106
  471.6 14.5 %scatter_fusion = f32[64,128,128]{2,1,0:T(8,128)} fusion(f32[64,128,128]{2,1,0:T(8,128)} %get-tuple-element.337, s32[64]{0:T(128)S(1)} %fusion.82, f32[64,128,128]{2,1,0:T(8,128)} %bitcast.223), kind=kCustom, calls=%fused_computation.3.clone.clone.1 | custom fusion | flops 1048576 | bytes 12583168 | tf_op jit(solution)/shard_map/while/body/scatter-add | solution.py:105
  500.6 16.5 %scatter_fusion.1 = f32[64,128,128]{2,1,0:T(8,128)} fusion(f32[64,128,128]{2,1,0:T(8,128)} %get-tuple-element.338, s32[64]{0:T(128)S(1)} %fusion.82, f32[64,128,128]{2,1,0:T(8,128)} %bitcast.222), kind=kCustom, calls=%fused_computation.4.clone.clone.1 | custom fusion | flops 1048576 | bytes 12583168 | tf_op jit(solution)/shard_map/while/body/scatter-add | solution.py:106
  519.8 14.5 %scatter_fusion = f32[64,128,128]{2,1,0:T(8,128)} fusion(f32[64,128,128]{2,1,0:T(8,128)} %get-tuple-element.337, s32[64]{0:T(128)S(1)} %fusion.82, f32[64,128,128]{2,1,0:T(8,128)} %bitcast.223), kind=kCustom, calls=%fused_computation.3.clone.clone.1 | custom fusion | flops 1048576 | bytes 12583168 | tf_op jit(solution)/shard_map/while/body/scatter-add | solution.py:105
  534.2 8.3 %copy_bitcast_fusion = (f32[1,64,128,128]{3,1,2,0:T(8,128)S(1)}, f32[1,64,128,128]{3,1,2,0:T(8,128)S(1)}) fusion(f32[64,128,128]{2,1,0:T(8,128)} %get-tuple-element.85, f32[64,128,128]{2,1,0:T(8,128)} %get-tuple-element.84), kind=kLoop, calls=%fused_computation.54 | loop fusion | bytes 16777216 | tf_op jit(solution)/shard_map/reshape | solution.py:122
  542.6 15.3 %convert_bitcast_fusion = bf16[128,1,128,256]{0,3,2,1:T(8,128)(2,1)} fusion(f32[1,64,128,128]{3,1,2,0:T(8,128)S(1)} %get-tuple-element.221, f32[1,64,128,128]{3,1,2,0:T(8,128)S(1)} %get-tuple-element.222, s32[64]{0:T(128)S(1)} %add.138), kind=kOutput, calls=%fused_computation.53 | convolution fusion | flops 3227525120 | bytes 16777472 | tf_op jit(solution)/shard_map/gcb,gcsd->bgsd/dot_general | solution.py:130
  557.9 12.4 %copy.145 = bf16[128,1,128,256]{3,2,1,0:T(8,128)(2,1)} copy(bf16[128,1,128,256]{0,3,2,1:T(8,128)(2,1)} %convert_bitcast_fusion) | data formatting | bytes 16777216 | tf_op jit(solution)/shard_map/convert_element_type | solution.py:136
  572.2 20.3 %all_to_all.74 = bf16[8,32,1024]{2,1,0:T(8,128)(2,1)S(1)} all-to-all(bf16[8,32,1024]{2,1,0:T(8,128)(2,1)S(1)} %all_to_all.64), channel_id=1, replica_groups=mesh['seq'=32,'kv'=8] {'kv'}, dimensions={0} | all-to-all | bytes 1048576 | tf_op jit(solution)/shard_map/all_to_all | solution.py:117
  593.4 73.0 %reduce-scatter.2.cloned.1.call-done = bf16[4,1,128,256]{3,2,1,0:T(8,128)(2,1)} async-done(((bf16[128,1,128,256]{3,2,1,0:T(8,128)(2,1)}), bf16[4,1,128,256]{3,2,1,0:T(8,128)(2,1)}) %reduce-scatter.2.cloned.1.call-update) | async-done | bytes 262160 | tf_op jit(solution)/shard_map/reduce_scatter | solution.py:129
  (269 shorter events, 166.0 us)
Async XLA Ops:
  7.2 48.3 %copy-start.4 = (bf16[32,8192]{1,0:T(8,128)(2,1)S(1)}, bf16[32,8192]{1,0:T(8,128)(2,1)}, u32[]{:S(2)}) copy-start(bf16[32,8192]{1,0:T(8,128)(2,1)} %param.12) | copy-start | bytes 1572868
  7.2 69.7 %copy-start.7 = (bf16[1,512,128]{2,1,0:T(8,128)(2,1)S(1)}, bf16[1,512,128]{2,1,0:T(8,128)(2,1)}, u32[]{:S(2)}) copy-start(bf16[1,512,128]{2,1,0:T(8,128)(2,1)} %param.15) | copy-start | bytes 393220
  7.2 69.7 %copy-start.8 = (bf16[1,512,128]{2,1,0:T(8,128)(2,1)S(1)}, bf16[1,512,128]{2,1,0:T(8,128)(2,1)}, u32[]{:S(2)}) copy-start(bf16[1,512,128]{2,1,0:T(8,128)(2,1)} %param.14) | copy-start | bytes 393220
  10.4 15.5 %all-to-all-start = ((s32[1,32,2]{2,0,1:T(1,128)}), s32[1,32,2]{2,0,1:T(1,128)S(1)}, u32[]{:S(2)}, u32[]{:S(2)}) async-start(s32[1,32,2]{2,0,1:T(1,128)} %copy.132), calls=%async_computation | async-start | bytes 32768 | tf_op jit(solution)/shard_map/all_to_all | solution.py:51
  25.9 26.1 %all-to-all-start.2 = ((bf16[32,8,1024]{2,0,1:T(8,128)(2,1)}), bf16[32,8,1024]{2,0,1:T(8,128)(2,1)S(1)}, u32[]{:S(2)}, u32[]{:S(2)}) async-start(bf16[32,8,1024]{2,0,1:T(8,128)(2,1)} %bitcast.173), calls=%async_computation.2 | async-start | bytes 1048576 | tf_op jit(solution)/shard_map/all_to_all | solution.py:29
  52.0 21.4 %all-to-all-start.4 = ((bf16[32,8,1024]{2,0,1:T(8,128)(2,1)}), bf16[32,8,1024]{2,0,1:T(8,128)(2,1)S(1)}, u32[]{:S(2)}, u32[]{:S(2)}) async-start(bf16[32,8,1024]{2,0,1:T(8,128)(2,1)} %bitcast.171), calls=%async_computation.4 | async-start | bytes 1048576 | tf_op jit(solution)/shard_map/all_to_all | solution.py:30
  73.4 21.4 %all-to-all-start.3 = ((bf16[32,8,1024]{2,0,1:T(8,128)(2,1)}), bf16[32,8,1024]{2,0,1:T(8,128)(2,1)S(1)}, u32[]{:S(2)}, u32[]{:S(2)}) async-start(bf16[32,8,1024]{2,0,1:T(8,128)(2,1)} %bitcast.172), calls=%async_computation.3 | async-start | bytes 1048576 | tf_op jit(solution)/shard_map/all_to_all | solution.py:31
  94.8 5.1 copy-start.9
  94.8 6.4 copy-start.6
  94.8 57.4 %all-to-all-start.1 = ((bf16[1,32,2,128,256]{4,3,2,0,1:T(8,128)(2,1)}), bf16[1,32,2,128,256]{4,3,2,0,1:T(8,128)(2,1)}, u32[]{:S(2)}, u32[]{:S(2)}) async-start(bf16[1,32,2,128,256]{4,3,2,0,1:T(8,128)(2,1)} %bitcast.228), calls=%async_computation.1 | async-start | bytes 8388608 | tf_op jit(solution)/shard_map/all_to_all | solution.py:58
  99.8 566.6 %reduce-scatter.2.cloned.1.call-start = ((), (), s32[]{:S(2)}) async-start(), calls=%async_computation.7 | async-start | bytes 8650752 | tf_op jit(solution)/shard_map/reduce_scatter | solution.py:129
  153.2 5.0 copy-start.5
  163.8 2.8 copy-start
  166.6 1.8 copy-start.1
  169.5 3.2 copy-start.2
  207.8 2.8 copy-start
  210.6 1.8 copy-start.1
  213.5 3.2 copy-start.2
  252.9 2.8 copy-start
  258.6 3.2 copy-start.2
  299.9 2.8 copy-start
  302.7 1.8 copy-start.1
  305.6 3.2 copy-start.2
  347.4 2.8 copy-start
  350.2 1.9 copy-start.1
  353.2 3.2 copy-start.2
  395.6 2.8 copy-start
  401.3 3.2 copy-start.2
  443.6 2.8 copy-start
  449.4 3.2 copy-start.2
  491.7 2.8 copy-start
  497.5 3.2 copy-start.2
  (5 other events, 8.6 us)
Sparse Core Ops, SparseCore 0:
  570.5 95.9 reduce-scatter.1
where the time goes:
time: 680 us; the launch traced here: 676 us
  other arithmetic  246 us (36%)
  waiting for transfers between devices  168 us (25%)
  matrix products  104 us (15%)
  local copies, waits for them, and re-layouts  92.9 us (14%)
  starting transfers between devices  28.9 us (4%)
  blocking collectives  20.3 us (3%)
  between operations  15 us (2%)
    scatter-add x8, other arithmetic, one_round(): grad_v = grad_v.at[flat_slots].add(value_terms.reshape(-1, BLK, head_dim))  125 us
    scatter-add x8, other arithmetic, one_round(): grad_k = grad_k.at[flat_slots].add(key_terms.reshape(-1, BLK, head_dim))  113 us
    reduce_scatter x1, waiting for transfers between devices, on_device(): lax.psum_scatter(jnp.einsum('gcb,gcsd->bgsd', selector, slot_pairs, preci...  73 us
    all_to_all x1, waiting for transfers between devices, on_device(): lax.all_to_all(served, 'seq', split_axis=1, concat_axis=1, tiled=True)  43 us
    gather x8, local copies, waits for them, and re-layouts, one_round(): tile_pairs = fetched[slot_rows]  39.6 us
    dot_general x8, matrix products, one_round(): jnp.einsum('ghqjts,qtghd->ghqjsd', weights_half, grad_five, preferred_ele...  25.2 us
    dot_general x8, matrix products, one_round(): jnp.einsum('ghqjts,qtghd->ghqjsd', scores_half, query_five, preferred_ele...  21.2 us
    all_to_all x1, blocking collectives, on_device(): lax.all_to_all(query_grad, 'kv', split_axis=0, concat_axis=1, tiled=True)  20.3 us
  transfers between devices with their start and end apart: 6, of which 6 were waited for; matrix products, arithmetic and copies ran while one was open for 3% of the time, Pallas kernels for 0%

commit v1 on v0

v1 whole, which is shorter than its diff:
```python
import math

import jax
import jax.numpy as jnp
from jax import lax
from jax.experimental import pallas as pl
from jax.experimental.pallas import tpu as pltpu
from jax.sharding import PartitionSpec as P

MESH = pl.DeviceIdType.MESH

G = 4
BLK = 128
LOG2E = math.log2(math.e)

def grads_kernel(lists, counts, q_ref, do_ref, lse_ref, dp_ref, k_ref, v_ref, dq_ref, dk_ref, dv_ref, acc, w1, w2, rowv, dqa):
    scale = 1.0 / math.sqrt(128.0)
    f32, bf = jnp.float32, jnp.bfloat16

    def zero(i, _):
        acc[i] = jnp.zeros((BLK, 256), f32)
        return 0
    lax.fori_loop(0, 128, zero, 0)
    w1[...] = jnp.zeros((256, 256), bf)
    w2[...] = jnp.zeros((256, 256), bf)
    for qb in range(2):
        d = dp_ref[4 * qb]
        for s in range(1, 4):
            d = d + pltpu.roll(dp_ref[4 * qb + s], 32 * s, 1)
        rowv[0, qb] = d
        rowv[1, qb] = lse_ref[:, qb * BLK:(qb + 1) * BLK] * LOG2E
    rows_i = lax.broadcasted_iota(jnp.int32, (BLK, BLK), 0)
    cols_i = lax.broadcasted_iota(jnp.int32, (BLK, BLK), 1)

    def one_row(r, _):
        h, qb = r // 2, lax.rem(r, 2)
        cs = pl.ds(pl.multiple_of(h * BLK, BLK), BLK)
        rs = pl.ds(pl.multiple_of(qb * BLK, BLK), BLK)
        q = q_ref[rs, cs]
        d = do_ref[rs, cs]
        w1[:BLK, :BLK] = q.T
        w1[BLK:, BLK:] = d.T
        w2[:BLK, :BLK] = q
        w2[BLK:, BLK:] = d
        dqa[...] = jnp.zeros((BLK, BLK), f32)
        delta = rowv[0, qb, pl.ds(h, 1), :]
        lse2 = rowv[1, qb, pl.ds(h, 1), :]
        count = counts[h, qb]

        def group(g, _):
            j0 = g * G
            bs = [lists[h, qb, j0 + i] for i in range(G)]
            ks = [k_ref[b] for b in bs]
            kv = jnp.concatenate([jnp.concatenate([ks[i], v_ref[bs[i]]], axis=1) for i in range(G)], axis=0)
            sd = jnp.dot(kv, w1[...], preferred_element_type=f32)
            dss, pds = [], []
            for i in range(G):
                s = sd[i * BLK:(i + 1) * BLK, :BLK]
                dpv = sd[i * BLK:(i + 1) * BLK, BLK:]
                bias = jnp.where(j0 + i < count, lse2, 1e30)
                p = jnp.exp2(s * (scale * LOG2E) - bias)
                if i == 0:
                    p = jnp.where((rows_i <= cols_i) | (g > 0), p, 0.0)
                ds = p * (dpv - delta)
                dsb = ds.astype(bf)
                dss.append(dsb)
                pds.append(jnp.concatenate([dsb, p.astype(bf)], axis=1))
            out = jnp.dot(jnp.concatenate(pds, axis=0), w2[...], preferred_element_type=f32)
            dst = jnp.concatenate([x.T for x in dss], axis=1)
            dqa[...] += jnp.dot(dst, jnp.concatenate(ks, axis=0), preferred_element_type=f32)
            for i in range(G):
                acc[bs[i]] += out[i * BLK:(i + 1) * BLK]
            return 0
        lax.fori_loop(0, (count + (G - 1)) // G, group, 0)
        dq_ref[rs, cs] = (dqa[...] * scale).astype(bf)
        return 0
    lax.fori_loop(0, 16, one_row, 0)

    def fin(i, _):
        a = acc[i]
        dk_ref[i] = a[:, :BLK].astype(bf)
        dv_ref[i] = a[:, BLK:].astype(bf)
        return 0
    lax.fori_loop(0, 128, fin, 0)

def grads(lists, counts, q, do, lse, dp, k, v):
    V = pl.BlockSpec(memory_space=pltpu.VMEM)
    S = pl.BlockSpec(memory_space=pltpu.SMEM)
    bf = jnp.bfloat16
    return pl.pallas_call(grads_kernel,
        out_shape=(jax.ShapeDtypeStruct((256, 1024), bf), jax.ShapeDtypeStruct((128, 128, 128), bf), jax.ShapeDtypeStruct((128, 128, 128), bf)),
        in_specs=[S, S] + [V] * 6, out_specs=(V, V, V),
        scratch_shapes=[pltpu.VMEM((128, 128, 256), jnp.float32), pltpu.VMEM((256, 256), bf), pltpu.VMEM((256, 256), bf), pltpu.VMEM((2, 2, 8, 128), jnp.float32), pltpu.VMEM((128, 128), jnp.float32)],
        compiler_params=pltpu.CompilerParams(vmem_limit_bytes=56 * 2**20))(lists, counts, q, do, lse, dp, k, v)


class Wires:
    def __init__(self, send_sem, recv_sem, local_sem):
        self.send_sem, self.recv_sem, self.local_sem = send_sem, recv_sem, local_sem
        self.count = 0
        self.local_count = 0
        self.started = []

    def send(self, src, dst, device):
        i = self.count
        self.count += 1
        copy = pltpu.make_async_remote_copy(
            src_ref=src,
            dst_ref=dst,
            send_sem=self.send_sem.at[i],
            recv_sem=self.recv_sem.at[i],
            device_id=device,
            device_id_type=MESH,
        )
        copy.start()
        self.started.append(copy)
        return copy

    def local(self, src, dst):
        i = self.local_count
        self.local_count += 1
        copy = pltpu.make_async_copy(src, dst, self.local_sem.at[i])
        copy.start()
        return copy

    def finish_sends(self):
        for copy in self.started:
            copy.wait_send()


def greet(devices):
    barrier = pltpu.get_barrier_semaphore()
    for device in devices:
        pl.semaphore_signal(barrier, inc=1, device_id=device, device_id_type=MESH)
    pl.semaphore_wait(barrier, len(devices))


def place():
    s = lax.axis_index("seq")
    x, y, c = s // 8, lax.rem(s // 2, 4), lax.rem(s, 2)

    def at(dx, dy, other=0):
        core = c if other == 0 else 1 - c
        return {"seq": (lax.rem(x + dx + 4, 4) * 4 + lax.rem(y + dy + 4, 4)) * 2 + core}

    return x, y, c, at


def wrap4(i):
    return lax.rem(i + 4, 4)


def spread_kernel(
    q_ref, o_ref, g_ref, k_ref, v_ref,
    qo_ref, go_ref, dp_ref, kf_ref, vf_ref,
    o_buf, g_buf, d_buf, send_sem, recv_sem, local_sem,
):
    me = lax.axis_index("kv")
    x, y, c, at = place()
    z_at = [{"kv": lax.rem(me + i, 8)} for i in range(8)]
    greet(z_at[1:] + [at(1, 0), at(-1, 0), at(0, 1), at(0, -1), at(0, 0, 1)])
    wires = Wires(send_sem, recv_sem, local_sem)
    locals_ = []
    waits = []

    load_o = wires.local(o_ref, o_buf)
    load_g = wires.local(g_ref, g_buf)

    class Ring:
        def __init__(self, src, full, x_first):
            self.src, self.full, self.x_first = src, full, x_first

        def dev(self, da, db):
            return at(da, db) if self.x_first else at(db, da)

        def slot(self, da, db, half=None):
            dx, dy = (da, db) if self.x_first else (db, da)
            ref = self.full.at[wrap4(x + dx), wrap4(y + dy), c]
            return ref if half is None else ref.at[pl.ds(half * 256, 256)]

        def put(self, ref, da, db):
            return wires.send(ref, ref, self.dev(da, db))

        def share(self, da, db):
            ref = self.slot(da, db)
            waits.append(wires.send(ref, ref, at(0, 0, 1)))

        def begin(self):
            own = self.slot(0, 0)
            self.ap = wires.send(self.src, own, self.dev(1, 0))
            self.am = wires.send(self.src, own, self.dev(-1, 0))
            self.bp = [wires.send(self.src, own, self.dev(0, 1))]
            self.bm = [wires.send(self.src, own, self.dev(0, -1))]

        def own(self):
            own = self.slot(0, 0)
            waits.append(wires.send(self.src, own, at(0, 0, 1)))
            locals_.append(wires.local(self.src, own))

        def both(self, ref):
            self.bp.append(self.put(ref, 0, 1))
            self.bm.append(self.put(ref, 0, -1))

        def first(self):
            self.ap.wait_recv()
            self.a2p = self.put(self.slot(-1, 0, 0), 1, 0)
            self.both(self.slot(-1, 0))
            self.am.wait_recv()
            self.a2m = self.put(self.slot(1, 0, 1), -1, 0)
            self.both(self.slot(1, 0))
            self.share(-1, 0)
            self.share(1, 0)

        def second(self):
            self.a2p.wait_recv()
            self.both(self.slot(2, 0, 0))
            self.a2m.wait_recv()
            self.both(self.slot(2, 0, 1))
            self.share(2, 0)

        def third(self, step):
            if step == 0:
                self.bp[0].wait_recv()
                self.c = [self.put(self.slot(0, -1), 0, 1)]
                self.share(0, -1)
                self.bm[0].wait_recv()
                self.share(0, 1)
            elif step == 1:
                self.bp[1].wait_recv()
                self.c.append(self.put(self.slot(-1, -1), 0, 1))
                self.share(-1, -1)
                self.bm[1].wait_recv()
                self.share(-1, 1)
            elif step == 2:
                self.bp[2].wait_recv()
                self.share(1, -1)
                self.bm[2].wait_recv()
                self.c.append(self.put(self.slot(1, 1), 0, -1))
                self.share(1, 1)
            else:
                self.bm[3].wait_recv()
                self.c.append(self.put(self.slot(2, 1, 0), 0, -1))
                self.bm[4].wait_recv()
                self.c.append(self.put(self.slot(2, 1, 1), 0, -1))
                self.share(2, 1)
                self.bp[3].wait_recv()
                self.bp[4].wait_recv()
                self.share(2, -1)

        def fourth(self, step):
            if step < 3:
                self.c[step].wait_recv()
                self.share((0, -1, 1)[step], 2)
            else:
                self.c[3].wait_recv()
                self.c[4].wait_recv()
                self.share(2, 2)

    rings = (Ring(k_ref, kf_ref, True), Ring(v_ref, vf_ref, False))
    for ring in rings:
        ring.begin()
    rows = pl.ds(pl.multiple_of(me * 32, 32), 32)

    def columns(i):
        return pl.ds(pl.multiple_of(lax.rem(me + i, 8) * 1024, 1024), 1024)

    for i in (4, 3, 5, 2, 6, 1, 7):
        for src, dst in ((q_ref, qo_ref), (g_ref, go_ref)):
            waits.append(wires.send(src.at[:, columns(i)], dst.at[rows, :], z_at[i]))
    for src, dst in ((q_ref, qo_ref), (g_ref, go_ref)):
        locals_.append(wires.local(src.at[:, columns(0)], dst.at[rows, :]))
    for ring in rings:
        ring.own()

    load_o.wait()
    load_g.wait()
    of_head = (
        lax.broadcasted_iota(jnp.int32, (8, 1024), 1) // 128
        == lax.broadcasted_iota(jnp.int32, (8, 1024), 0)
    ).astype(jnp.float32)
    d_buf[...] = jnp.zeros(d_buf.shape, jnp.float32)
    for group in range(8):
        cols = pl.ds(group * 1024, 1024)
        terms = o_buf[:, cols].astype(jnp.float32) * g_buf[:, cols].astype(jnp.float32)
        d_buf[group, :, :32] = lax.dot_general(
            of_head,
            terms,
            (((1,), (1,)), ((), ())),
            precision=lax.Precision.HIGHEST,
            preferred_element_type=jnp.float32,
        )
    for i in range(1, 8):
        waits.append(wires.send(d_buf.at[lax.rem(me + i, 8)], dp_ref.at[me], z_at[i]))
    locals_.append(wires.local(d_buf.at[me], dp_ref.at[me]))

    for ring in rings:
        ring.first()
    for ring in rings:
        ring.second()
    for step in range(4):
        for ring in rings:
            ring.third(step)
    for step in range(4):
        for ring in rings:
            ring.fourth(step)
    for copy in waits:
        copy.wait_recv()
    for copy in locals_:
        copy.wait()
    wires.finish_sends()


def collect_kernel(
    dq_ref, dk_ref, dv_ref,
    gq_ref, gk_ref, gv_ref,
    mine_k, mine_v, sib_k, sib_v, far_k, far_v, near_k, near_v, end_k, end_v,
    send_sem, recv_sem, local_sem,
):
    me = lax.axis_index("kv")
    x, y, c, at = place()
    z_at = [{"kv": lax.rem(me + i, 8)} for i in range(8)]
    greet(z_at[1:] + [at(1, 0), at(-1, 0), at(0, 1), at(0, -1), at(0, 0, 1)])
    wires = Wires(send_sem, recv_sem, local_sem)
    f32, bf16 = jnp.float32, jnp.bfloat16
    waits = []

    class Ring:
        def __init__(self, src, mine, sib, far, near, end, x_first):
            self.src, self.mine, self.sib = src, mine, sib
            self.far, self.near, self.end, self.x_first = far, near, end, x_first
            self.a, self.b = (x, y) if x_first else (y, x)

        def dev(self, da, db):
            return at(da, db) if self.x_first else at(db, da)

        def line(self, ref, db, core=None):
            b = wrap4(self.b + db)
            at_ = (slice(None), b) if self.x_first else (b, slice(None))
            return ref.at[at_] if core is None else ref.at[at_ + (core,)]

        def cell(self, ref, da, db):
            a, b = wrap4(self.a + da), wrap4(self.b + db)
            return ref.at[a, b] if self.x_first else ref.at[b, a]

        def begin(self, db):
            load = wires.local(self.line(self.src, db, c), self.line(self.mine, db))
            swap = wires.send(
                self.line(self.src, db, 1 - c), self.line(self.sib, db), at(0, 0, 1)
            )
            return load, swap

        def begin_all(self):
            self.swaps = {db: self.begin(db) for db in (2, 1, -1, 0)}

        def join(self, db):
            load, swap = self.swaps[db]
            load.wait()
            swap.wait_recv()
            for da in (2, 1, -1, 0):
                m = self.cell(self.mine, da, db)
                s = self.cell(self.sib, da, db)
                m[...] = (m[...].astype(f32) + s[...].astype(f32)).astype(bf16)

        def one(self):
            self.join(2)
            self.far_p = [
                wires.send(self.cell(self.mine, da, 2), self.far.at[0, i], self.dev(0, 1))
                for i, da in enumerate((2, 1))
            ]
            self.far_m = [
                wires.send(self.cell(self.mine, da, 2), self.far.at[1, i], self.dev(0, -1))
                for i, da in enumerate((-1, 0))
            ]

        def two(self):
            self.near_p, self.near_m = {}, {}
            self.join(1)
            for da in (-1, 0):
                self.near_p[da] = wires.send(
                    self.cell(self.mine, da, 1), self.near.at[0, da % 4], self.dev(0, 1)
                )
            self.join(-1)
            for da in (2, 1):
                self.near_m[da] = wires.send(
                    self.cell(self.mine, da, -1), self.near.at[1, da % 4], self.dev(0, -1)
                )

        def three(self, i):
            da = (2, 1)[i]
            self.far_p[i].wait_recv()
            m = self.cell(self.mine, da, 1)
            m[...] = (m[...].astype(f32) + self.far[0, i].astype(f32)).astype(bf16)
            self.near_p[da] = wires.send(m, self.near.at[0, da % 4], self.dev(0, 1))
            da = (-1, 0)[i]
            self.far_m[i].wait_recv()
            m = self.cell(self.mine, da, -1)
            m[...] = (m[...].astype(f32) + self.far[1, i].astype(f32)).astype(bf16)
            self.near_m[da] = wires.send(m, self.near.at[1, da % 4], self.dev(0, -1))

        def total(self, da):
            self.near_p[da].wait_recv()
            self.near_m[da].wait_recv()
            m = self.cell(self.mine, da, 0)
            return (
                m[...].astype(f32)
                + self.near[0, da % 4].astype(f32)
                + self.near[1, da % 4].astype(f32)
            )

        def four(self):
            m = self.cell(self.mine, 2, 0)
            m[...] = self.total(2).astype(bf16)
            lo, hi = pl.ds(0, 256), pl.ds(256, 256)
            self.end_far_p = wires.send(m.at[lo], self.end.at[0, lo], self.dev(1, 0))
            self.end_far_m = wires.send(m.at[hi], self.end.at[0, hi], self.dev(-1, 0))

        def five(self):
            lo, hi = pl.ds(0, 256), pl.ds(256, 256)
            mp = self.cell(self.mine, 1, 0)
            mm = self.cell(self.mine, -1, 0)
            tp = self.total(1)
            mp[...] = tp.astype(bf16)
            tm = self.total(-1)
            mm[...] = tm.astype(bf16)
            self.end_far_p.wait_recv()
            mp[:256] = (mp[:256].astype(f32) + self.end[0, :256].astype(f32)).astype(bf16)
            self.end_p = wires.send(mp, self.end.at[1], self.dev(1, 0))
            self.end_far_m.wait_recv()
            mm[256:] = (mm[256:].astype(f32) + self.end[0, 256:].astype(f32)).astype(bf16)
            self.end_m = wires.send(mm, self.end.at[2], self.dev(-1, 0))

        def six(self, out, scale):
            t = self.total(0)
            self.end_p.wait_recv()
            self.end_m.wait_recv()
            t = t + self.end[1].astype(f32) + self.end[2].astype(f32)
            out[...] = (t * scale).astype(bf16)

    rings = (
        Ring(dk_ref, mine_k, sib_k, far_k, near_k, end_k, True),
        Ring(dv_ref, mine_v, sib_v, far_v, near_v, end_v, False),
    )
    for db in (2, 1, -1, 0):
        for ring in rings:
            if db == 2:
                ring.swaps = {}
            ring.swaps[db] = ring.begin(db)

    def rows(i):
        return pl.ds(pl.multiple_of(lax.rem(me + i, 8) * 32, 32), 32)

    cols = pl.ds(pl.multiple_of(me * 1024, 1024), 1024)
    for i in (4, 3, 5, 2, 6, 1, 7):
        waits.append(wires.send(dq_ref.at[rows(i), :], gq_ref.at[:, cols], z_at[i]))
    own = wires.local(dq_ref.at[rows(0), :], gq_ref.at[:, cols])
    for ring in rings:
        ring.one()
    for ring in rings:
        ring.two()
    for i in range(2):
        for ring in rings:
            ring.three(i)
    for ring in rings:
        ring.join(0)
    for ring in rings:
        ring.four()
    for ring in rings:
        ring.five()
    rings[0].six(gk_ref, 1.0 / math.sqrt(128.0))
    rings[1].six(gv_ref, 1.0)
    for copy in waits:
        copy.wait_recv()
    own.wait()
    wires.finish_sends()


ANY = pl.BlockSpec(memory_space=pl.ANY)
VM = pl.BlockSpec(memory_space=pltpu.VMEM)
SM = pl.BlockSpec(memory_space=pltpu.SMEM)
DMA = pltpu.SemaphoreType.DMA


def spread(q, o, g, k, v):
    bf16 = jnp.bfloat16
    rows = jax.ShapeDtypeStruct((256, 1024), bf16)
    cache = jax.ShapeDtypeStruct((4, 4, 2, 512, 128), bf16)
    return pl.pallas_call(
        spread_kernel,
        out_shape=(rows, rows, jax.ShapeDtypeStruct((8, 8, 128), jnp.float32), cache, cache),
        in_specs=[ANY] * 5,
        out_specs=(ANY,) * 5,
        scratch_shapes=[
            pltpu.VMEM((32, 8192), bf16),
            pltpu.VMEM((32, 8192), bf16),
            pltpu.VMEM((8, 8, 128), jnp.float32),
            DMA((96,)),
            DMA((96,)),
            DMA((8,)),
        ],
        compiler_params=pltpu.CompilerParams(
            collective_id=0, has_side_effects=True, vmem_limit_bytes=16 * 2**20
        ),
    )(q, o, g, k, v)


def collect(dq, dk, dv):
    bf16 = jnp.bfloat16
    out = jax.ShapeDtypeStruct((512, 128), bf16)
    return pl.pallas_call(
        collect_kernel,
        out_shape=(jax.ShapeDtypeStruct((32, 8192), bf16), out, out),
        in_specs=[ANY] * 3,
        out_specs=(ANY, VM, VM),
        scratch_shapes=[
            pltpu.VMEM((4, 4, 512, 128), bf16),
            pltpu.VMEM((4, 4, 512, 128), bf16),
            pltpu.VMEM((4, 4, 512, 128), bf16),
            pltpu.VMEM((4, 4, 512, 128), bf16),
            pltpu.VMEM((2, 2, 512, 128), bf16),
            pltpu.VMEM((2, 2, 512, 128), bf16),
            pltpu.VMEM((2, 4, 512, 128), bf16),
            pltpu.VMEM((2, 4, 512, 128), bf16),
            pltpu.VMEM((3, 512, 128), bf16),
            pltpu.VMEM((3, 512, 128), bf16),
            DMA((64,)),
            DMA((64,)),
            DMA((16,)),
        ],
        compiler_params=pltpu.CompilerParams(
            collective_id=1, has_side_effects=True, vmem_limit_bytes=40 * 2**20
        ),
    )(dq, dk, dv)


def on_device(
    query_rows, attn_out, grad_out, logsumexp, key_cache, value_cache, block_lists, block_counts
):
    q, g, dp, kf, vf = spread(query_rows, attn_out, grad_out, key_cache[0], value_cache[0])
    blocks = (128, 128, 128)
    dq, dk, dv = grads(
        block_lists, block_counts, q, g, logsumexp, dp, kf.reshape(blocks), vf.reshape(blocks)
    )
    gq, gk, gv = collect(dq, dk.reshape(kf.shape), dv.reshape(vf.shape))
    return gq, gk[None], gv[None]


def solution(mesh):
    placed = (
        P(("seq", "kv"), None),
        P(("seq", "kv"), None),
        P(("seq", "kv"), None),
        P("kv", "seq"),
        P("kv", "seq", None),
        P("kv", "seq", None),
        P("kv", "seq", None),
        P("kv", "seq"),
    )
    return jax.shard_map(
        on_device,
        mesh=mesh,
        in_specs=placed,
        out_specs=(P(("seq", "kv"), None), P("kv", "seq", None), P("kv", "seq", None)),
        check_vma=False,
    )
```

time: 680 us -> 130 us (0.19)
  the two profiles are of different devices: /device:TPU:1 before, /device:TPU:2 now
where the time goes in v1:
time: 130 us; the launch traced here: 129 us
  Pallas kernels  109 us (84%)
  local copies, waits for them, and re-layouts  19.9 us (15%)
    pallas_call x1, Pallas kernels, collect(): pl.pallas_call(collect_kernel, out_shape=(jax.ShapeDtypeStruct((32, 8192)...  42.7 us
    pallas_call x1, Pallas kernels, spread(): pl.pallas_call(spread_kernel, out_shape=(rows, rows, jax.ShapeDtypeStruct...  36.5 us
    pallas_call x1, Pallas kernels, grads(): pl.pallas_call(grads_kernel, out_shape=(jax.ShapeDtypeStruct((256, 1024),...  29.4 us
    unnamed x30, local copies, waits for them, and re-layouts  19.9 us

profile of v1, /device:TPU:2, one launch (start us, length us, event | category | flops | bytes accessed | tf_op | source)
XLA Modules:
  0.0 129.1 jit_solution(1724877502255878716)
XLA Ops:
  0.6 1.3 %copy.11.counts = s32[8,2]{1,0:T(8,128)} copy(s32[8,2]{0,1:T(2,128)} %param.15) | data formatting | bytes 128 | tf_op args[7]
  2.0 0.0 copy-start.4
  2.0 1.0 copy-done.4
  3.0 0.0 copy-start.5
  3.0 1.0 copy-done.5
  4.1 0.0 copy-start.6
  4.1 1.0 copy-done.6
  5.1 0.0 copy-start.10
  5.1 0.9 copy-done.10
  6.0 0.0 copy-start.11
  6.0 0.9 copy-done.11
  6.9 36.5 %shard_map.103 = (bf16[256,1024]{1,0:T(8,128)(2,1)S(1)}, bf16[256,1024]{1,0:T(8,128)(2,1)S(1)}, f32[8,8,128]{2,1,0:T(8,128)S(1)}, bf16[4,4,2,512,128]{4,3,2,1,0:...) custom-call(bf16[32,8192]{1,0:T(8,128)(2,1)S(1)} %copy-done.4, bf16[32,8192]{1,0:T(8,128)(2,1)S(1)} %copy-done.5, ...), custom_call_target="tpu_custom_call" | custom-call | tf_op jit(solution)/shard_map/pallas_call | solution.py:487
  43.4 0.0 copy-start.2
  43.4 1.9 %copy-done.2 = bf16[4,4,2,512,128]{4,3,2,1,0:T(8,128)(2,1)} copy-done((bf16[4,4,2,512,128]{4,3,2,1,0:T(8,128)(2,1)}, bf16[4,4,2,512,128]{4,3,2,1,0:T(8,128)(2,1)S(1)}, u32[]{:S(2)}) %copy-start.2) | copy-done | bytes 4194328
  45.3 0.0 copy-start.3
  45.3 2.0 %copy-done.3 = bf16[4,4,2,512,128]{4,3,2,1,0:T(8,128)(2,1)} copy-done((bf16[4,4,2,512,128]{4,3,2,1,0:T(8,128)(2,1)}, bf16[4,4,2,512,128]{4,3,2,1,0:T(8,128)(2,1)S(1)}, u32[]{:S(2)}) %copy-start.3) | copy-done | bytes 4194328
  47.3 0.8 copy-done.8
  48.1 0.0 copy-start.9
  48.1 0.8 copy-done.9
  48.9 0.0 copy-start.12
  48.9 0.6 copy-done.12
  49.5 29.4 %shard_map.104 = (bf16[256,1024]{1,0:T(8,128)(2,1)}, bf16[128,128,128]{2,1,0:T(8,128)(2,1)}, bf16[128,128,128]{2,1,0:T(8,128)(2,1)}) custom-call(s32[8,2,32]{2,1,0:T(2,128)} %lists.1, s32[8,2]{1,0:T(8,128)} %copy.11.counts, bf16[256,1024]{1,0:T(8,128)(2,1)} %copy-done.8, bf16[256,1024]{1,0:T(8,128)(2,1)} %copy-done.9, f32[8,256]{1,0:T(8,128)} %lse_ref.1, ...), custom_call_target="tpu_custom_call" | custom-call | tf_op jit(solution)/shard_map/pallas_call | solution.py:90
  78.9 0.0 copy-start
  78.9 2.2 %copy-done = bf16[128,128,128]{2,1,0:T(8,128)(2,1)S(1)} copy-done((bf16[128,128,128]{2,1,0:T(8,128)(2,1)S(1)}, bf16[128,128,128]{2,1,0:T(8,128)(2,1)}, u32[]{:S(2)}) %copy-start) | copy-done | bytes 4194328
  81.1 0.0 copy-start.1
  81.1 2.2 %copy-done.1 = bf16[128,128,128]{2,1,0:T(8,128)(2,1)S(1)} copy-done((bf16[128,128,128]{2,1,0:T(8,128)(2,1)S(1)}, bf16[128,128,128]{2,1,0:T(8,128)(2,1)}, u32[]{:S(2)}) %copy-start.1) | copy-done | bytes 4194328
  83.3 0.0 copy-start.7
  83.3 1.0 copy-done.7
  84.3 42.7 %shard_map.105 = (bf16[32,8192]{1,0:T(8,128)(2,1)S(1)}, bf16[512,128]{1,0:T(8,128)(2,1)S(1)}, bf16[512,128]{1,0:T(8,128)(2,1)S(1)}) custom-call(bf16[256,1024]{1,0:T(8,128)(2,1)S(1)} %copy-done.7, bf16[4,4,2,512,128]{4,3,2,1,0:T(8,128)(2,1)S(1)} %bitcast.8, bf16[4,4,2,512,128]{4,3,2,1,0:T(8,128)(2,1)S(1)} %bitcast.9), custom_call_target="tpu_custom_call" | custom-call | tf_op jit(solution)/shard_map/pallas_call | solution.py:509
  127.0 0.8 copy.15
  127.8 0.7 copy.16
  128.5 0.7 copy.17
  (1 shorter events, 0.0 us)
Async XLA Ops:
  2.0 1.0 copy-start.4
  3.0 1.0 copy-start.5
  4.1 1.0 copy-start.6
  5.1 0.9 copy-start.10
  6.0 0.9 copy-start.11
  43.4 2.0 %copy-start.2 = (bf16[4,4,2,512,128]{4,3,2,1,0:T(8,128)(2,1)}, bf16[4,4,2,512,128]{4,3,2,1,0:T(8,128)(2,1)S(1)}, u32[]{:S(2)}) copy-start(bf16[4,4,2,512,128]{4,3,2,1,0:T(8,128)(2,1)S(1)} %get-tuple-element.17) | copy-start | bytes 12582916
  45.3 2.0 %copy-start.3 = (bf16[4,4,2,512,128]{4,3,2,1,0:T(8,128)(2,1)}, bf16[4,4,2,512,128]{4,3,2,1,0:T(8,128)(2,1)S(1)}, u32[]{:S(2)}) copy-start(bf16[4,4,2,512,128]{4,3,2,1,0:T(8,128)(2,1)S(1)} %get-tuple-element.18) | copy-start | bytes 12582916
  47.3 0.8 copy-start.8
  48.1 0.8 copy-start.9
  48.9 0.6 copy-start.12
  78.9 2.2 %copy-start = (bf16[128,128,128]{2,1,0:T(8,128)(2,1)S(1)}, bf16[128,128,128]{2,1,0:T(8,128)(2,1)}, u32[]{:S(2)}) copy-start(bf16[128,128,128]{2,1,0:T(8,128)(2,1)} %get-tuple-element.20) | copy-start | bytes 12582916
  81.1 2.2 %copy-start.1 = (bf16[128,128,128]{2,1,0:T(8,128)(2,1)S(1)}, bf16[128,128,128]{2,1,0:T(8,128)(2,1)}, u32[]{:S(2)}) copy-start(bf16[128,128,128]{2,1,0:T(8,128)(2,1)} %get-tuple-element.21) | copy-start | bytes 12582916
  83.3 1.0 copy-start.7

commit v2 on v1

v2 whole, which is shorter than its diff:
```python
import math

import jax
import jax.numpy as jnp
from jax import lax
from jax.experimental import pallas as pl
from jax.experimental.pallas import tpu as pltpu
from jax.sharding import PartitionSpec as P

MESH = pl.DeviceIdType.MESH

G = 4
UNROLL = 4
BLK = 128
LOG2E = math.log2(math.e)


def grads_kernel(
    lists_hbm, counts_hbm, q_ref, do_ref, lse_hbm, dp_ref, k_ref, v_ref,
    dq_ref, dk_ref, dv_ref,
    acc, dqa, w1, w2, row_delta, row_lse, slot_a, slot_b, row_of, at_of, lists, counts, lse_ref, sem,
):
    scale = 1.0 / math.sqrt(128.0)
    f32, bf16 = jnp.float32, jnp.bfloat16

    copies = [
        pltpu.make_async_copy(src, dst, sem.at[i])
        for i, (src, dst) in enumerate(
            ((counts_hbm, counts), (lists_hbm, lists), (lse_hbm, lse_ref))
        )
    ]
    for copy in copies:
        copy.start()

    def zero(i, _):
        acc[i] = jnp.zeros((BLK, 2 * BLK), f32)
        return 0

    lax.fori_loop(0, 128, zero, 0, unroll=4)

    for copy in copies:
        copy.wait()

    def list_row(r, n):
        def put(g, n):
            row_of[n] = r
            at_of[n] = g * G
            return n + 1

        return lax.fori_loop(0, (counts[lax.rem(r, 2), r // 2] + (G - 1)) // G, put, n)

    for i in range(UNROLL):
        row_of[i] = 0
        at_of[i] = 32
    total = lax.fori_loop(0, 16, list_row, UNROLL)
    for i in range(3 * UNROLL):
        row_of[total + i] = 0
        at_of[total + i] = 32

    for qb in range(2):
        d = dp_ref[4 * qb]
        for s in range(1, 4):
            d = d + pltpu.roll(dp_ref[4 * qb + s], 32 * s, 1)
        l = lse_ref[:, qb * BLK : (qb + 1) * BLK] * LOG2E
        for h in range(8):
            row_delta[2 * h + qb] = d[h : h + 1]
            row_lse[2 * h + qb] = l[h : h + 1]
    blank = jnp.zeros((BLK, BLK), bf16)

    def place_of(r):
        h, qb = r // 2, lax.rem(r, 2)
        return (
            pl.ds(pl.multiple_of(qb * BLK, BLK), BLK),
            pl.ds(pl.multiple_of(h * BLK, BLK), BLK),
        )

    def diagonal(a, b):
        return jnp.concatenate(
            [jnp.concatenate([a, blank], axis=1), jnp.concatenate([blank, b], axis=1)], axis=0
        )

    def prepare(r, _):
        q = q_ref[place_of(r)]
        d = do_ref[place_of(r)]
        w1[r] = diagonal(q.T, d.T)
        w2[r] = diagonal(q, d)
        dqa[r] = jnp.zeros((BLK, BLK), f32)
        return 0

    lax.fori_loop(0, 16, prepare, 0, unroll=4)
    causal = lax.broadcasted_iota(jnp.int32, (BLK, BLK), 0) <= lax.broadcasted_iota(
        jnp.int32, (BLK, BLK), 1
    )

    def where_of(n):
        r, first = row_of[n], at_of[n]
        h, qb = r // 2, lax.rem(r, 2)
        blocks = [lists[h, qb, jnp.minimum(first + i, 31)] for i in range(G)]
        return r, first, counts[qb, h], blocks

    def score(n, slot):
        r, _, _, blocks = where_of(n)
        pairs = [jnp.concatenate([k_ref[b], v_ref[b]], axis=1) for b in blocks]
        slot[...] = jnp.dot(jnp.concatenate(pairs, axis=0), w1[r], preferred_element_type=f32)

    def terms(n, slot):
        r, first, count, blocks = where_of(n)
        delta = row_delta[r]
        lse = row_lse[r]
        grad_scores, halves = [], []
        for i in range(G):
            s = slot[i * BLK : (i + 1) * BLK, :BLK]
            grad_weights = slot[i * BLK : (i + 1) * BLK, BLK:]
            bias = jnp.where(first + i < count, lse, 1e30)
            p = jnp.exp2(s * (scale * LOG2E) - bias)
            if i == 0:
                p = jnp.where(causal | (first > 0), p, 0.0)
            ds = (p * (grad_weights - delta)).astype(bf16)
            grad_scores.append(ds)
            halves.append(jnp.concatenate([ds, p.astype(bf16)], axis=1))
        out = jnp.dot(jnp.concatenate(halves, axis=0), w2[r], preferred_element_type=f32)
        dq = jnp.dot(
            jnp.concatenate([k_ref[b].T for b in blocks], axis=1),
            jnp.concatenate(grad_scores, axis=0),
            preferred_element_type=f32,
        )
        return r, blocks, out, dq

    def half(e, write, read):
        for u in range(UNROLL):
            score(e + UNROLL + u, write.at[u])
        for r, blocks, out, dq in [terms(e + u, read.at[u]) for u in range(UNROLL)]:
            dqa[r] += dq
            for i in range(G):
                acc[blocks[i]] += out[i * BLK : (i + 1) * BLK]

    def some_groups(m, _):
        half(2 * m * UNROLL, slot_a, slot_b)
        half((2 * m + 1) * UNROLL, slot_b, slot_a)
        return 0

    for u in range(UNROLL):
        slot_b[u] = jnp.zeros((G * BLK, 2 * BLK), f32)
    halves_needed = (total - UNROLL + UNROLL - 1) // UNROLL + 1
    lax.fori_loop(0, (halves_needed + 1) // 2, some_groups, 0)

    def finish_block(i, _):
        a = acc[i]
        dk_ref[i] = a[:, :BLK].astype(bf16)
        dv_ref[i] = a[:, BLK:].astype(bf16)
        return 0

    lax.fori_loop(0, 128, finish_block, 0, unroll=4)

    def finish_row(r, _):
        dq_ref[place_of(r)] = (dqa[r] * scale).astype(bf16).T
        return 0

    lax.fori_loop(0, 16, finish_row, 0, unroll=4)


def grads(lists, counts, q, do, lse, dp, k, v):
    vm = pl.BlockSpec(memory_space=pltpu.VMEM)
    hbm = pl.BlockSpec(memory_space=pltpu.HBM)
    bf16, f32 = jnp.bfloat16, jnp.float32
    return pl.pallas_call(
        grads_kernel,
        out_shape=(
            jax.ShapeDtypeStruct((256, 1024), bf16),
            jax.ShapeDtypeStruct((128, 128, 128), bf16),
            jax.ShapeDtypeStruct((128, 128, 128), bf16),
        ),
        in_specs=[hbm, hbm, vm, vm, hbm, vm, vm, vm],
        out_specs=(vm, vm, vm),
        scratch_shapes=[
            pltpu.VMEM((128, BLK, 2 * BLK), f32),
            pltpu.VMEM((16, BLK, BLK), f32),
            pltpu.VMEM((16, 2 * BLK, 2 * BLK), bf16),
            pltpu.VMEM((16, 2 * BLK, 2 * BLK), bf16),
            pltpu.VMEM((16, 1, BLK), f32),
            pltpu.VMEM((16, 1, BLK), f32),
            pltpu.VMEM((UNROLL, G * BLK, 2 * BLK), f32),
            pltpu.VMEM((UNROLL, G * BLK, 2 * BLK), f32),
            pltpu.SMEM((528,), jnp.int32),
            pltpu.SMEM((528,), jnp.int32),
            pltpu.SMEM((8, 2, 32), jnp.int32),
            pltpu.SMEM((2, 8), jnp.int32),
            pltpu.VMEM((8, 256), f32),
            pltpu.SemaphoreType.DMA((3,)),
        ],
        compiler_params=pltpu.CompilerParams(vmem_limit_bytes=36 * 2**20),
    )(lists, counts, q, do, lse, dp, k, v)


class Wires:
    def __init__(self, send_sem, recv_sem, local_sem):
        self.send_sem, self.recv_sem, self.local_sem = send_sem, recv_sem, local_sem
        self.count = 0
        self.local_count = 0
        self.started = []

    def send(self, src, dst, device):
        i = self.count
        self.count += 1
        copy = pltpu.make_async_remote_copy(
            src_ref=src,
            dst_ref=dst,
            send_sem=self.send_sem.at[i],
            recv_sem=self.recv_sem.at[i],
            device_id=device,
            device_id_type=MESH,
        )
        copy.start()
        self.started.append(copy)
        return copy

    def local(self, src, dst):
        i = self.local_count
        self.local_count += 1
        copy = pltpu.make_async_copy(src, dst, self.local_sem.at[i])
        copy.start()
        return copy

    def finish_sends(self):
        for copy in self.started:
            copy.wait_send()


def greet(devices):
    barrier = pltpu.get_barrier_semaphore()
    for device in devices:
        pl.semaphore_signal(barrier, inc=1, device_id=device, device_id_type=MESH)
    pl.semaphore_wait(barrier, len(devices))


def place():
    s = lax.axis_index("seq")
    x, y, c = s // 8, lax.rem(s // 2, 4), lax.rem(s, 2)

    def at(dx, dy, other=0):
        core = c if other == 0 else 1 - c
        return {"seq": (lax.rem(x + dx + 4, 4) * 4 + lax.rem(y + dy + 4, 4)) * 2 + core}

    return x, y, c, at


def wrap4(i):
    return lax.rem(i + 4, 4)


def spread_kernel(
    q_ref, o_ref, g_ref, k_ref, v_ref,
    qo_ref, go_ref, dp_ref, kf_ref, vf_ref,
    o_buf, g_buf, d_buf, send_sem, recv_sem, local_sem,
):
    me = lax.axis_index("kv")
    x, y, c, at = place()
    z_at = [{"kv": lax.rem(me + i, 8)} for i in range(8)]
    greet(z_at[1:] + [at(1, 0), at(-1, 0), at(0, 1), at(0, -1), at(0, 0, 1)])
    wires = Wires(send_sem, recv_sem, local_sem)
    locals_ = []
    waits = []

    load_o = wires.local(o_ref, o_buf)
    load_g = wires.local(g_ref, g_buf)

    class Ring:
        def __init__(self, src, full, x_first):
            self.src, self.full, self.x_first = src, full, x_first

        def dev(self, da, db):
            return at(da, db) if self.x_first else at(db, da)

        def slot(self, da, db, half=None):
            dx, dy = (da, db) if self.x_first else (db, da)
            ref = self.full.at[wrap4(x + dx), wrap4(y + dy), c]
            return ref if half is None else ref.at[pl.ds(half * 256, 256)]

        def put(self, ref, da, db):
            return wires.send(ref, ref, self.dev(da, db))

        def share(self, da, db):
            ref = self.slot(da, db)
            waits.append(wires.send(ref, ref, at(0, 0, 1)))

        def begin(self):
            own = self.slot(0, 0)
            self.ap = wires.send(self.src, own, self.dev(1, 0))
            self.am = wires.send(self.src, own, self.dev(-1, 0))
            self.bp = [wires.send(self.src, own, self.dev(0, 1))]
            self.bm = [wires.send(self.src, own, self.dev(0, -1))]

        def own(self):
            own = self.slot(0, 0)
            waits.append(wires.send(self.src, own, at(0, 0, 1)))
            locals_.append(wires.local(self.src, own))

        def both(self, ref):
            self.bp.append(self.put(ref, 0, 1))
            self.bm.append(self.put(ref, 0, -1))

        def first(self):
            self.ap.wait_recv()
            self.a2p = self.put(self.slot(-1, 0, 0), 1, 0)
            self.both(self.slot(-1, 0))
            self.am.wait_recv()
            self.a2m = self.put(self.slot(1, 0, 1), -1, 0)
            self.both(self.slot(1, 0))
            self.share(-1, 0)
            self.share(1, 0)

        def second(self):
            self.a2p.wait_recv()
            self.both(self.slot(2, 0, 0))
            self.a2m.wait_recv()
            self.both(self.slot(2, 0, 1))
            self.share(2, 0)

        def third(self, step):
            if step == 0:
                self.bp[0].wait_recv()
                self.c = [self.put(self.slot(0, -1), 0, 1)]
                self.share(0, -1)
                self.bm[0].wait_recv()
                self.share(0, 1)
            elif step == 1:
                self.bp[1].wait_recv()
                self.c.append(self.put(self.slot(-1, -1), 0, 1))
                self.share(-1, -1)
                self.bm[1].wait_recv()
                self.share(-1, 1)
            elif step == 2:
                self.bp[2].wait_recv()
                self.share(1, -1)
                self.bm[2].wait_recv()
                self.c.append(self.put(self.slot(1, 1), 0, -1))
                self.share(1, 1)
            else:
                self.bm[3].wait_recv()
                self.c.append(self.put(self.slot(2, 1, 0), 0, -1))
                self.bm[4].wait_recv()
                self.c.append(self.put(self.slot(2, 1, 1), 0, -1))
                self.share(2, 1)
                self.bp[3].wait_recv()
                self.bp[4].wait_recv()
                self.share(2, -1)

        def fourth(self, step):
            if step < 3:
                self.c[step].wait_recv()
                self.share((0, -1, 1)[step], 2)
            else:
                self.c[3].wait_recv()
                self.c[4].wait_recv()
                self.share(2, 2)

    rings = (Ring(k_ref.at[0], kf_ref, True), Ring(v_ref.at[0], vf_ref, False))
    for ring in rings:
        ring.begin()
    rows = pl.ds(pl.multiple_of(me * 32, 32), 32)

    def columns(i):
        return pl.ds(pl.multiple_of(lax.rem(me + i, 8) * 1024, 1024), 1024)

    for i in (1, 7, 2, 6, 3, 5, 4):
        for src, dst in ((q_ref, qo_ref), (g_ref, go_ref)):
            waits.append(wires.send(src.at[:, columns(i)], dst.at[rows, :], z_at[i]))
    for src, dst in ((q_ref, qo_ref), (g_ref, go_ref)):
        locals_.append(wires.local(src.at[:, columns(0)], dst.at[rows, :]))
    for ring in rings:
        ring.own()

    load_o.wait()
    load_g.wait()
    of_head = (
        lax.broadcasted_iota(jnp.int32, (8, 1024), 1) // 128
        == lax.broadcasted_iota(jnp.int32, (8, 1024), 0)
    ).astype(jnp.float32)
    d_buf[...] = jnp.zeros(d_buf.shape, jnp.float32)
    for group in range(8):
        cols = pl.ds(group * 1024, 1024)
        terms = o_buf[:, cols].astype(jnp.float32) * g_buf[:, cols].astype(jnp.float32)
        d_buf[group, :, :32] = lax.dot_general(
            of_head,
            terms,
            (((1,), (1,)), ((), ())),
            precision=lax.Precision.HIGHEST,
            preferred_element_type=jnp.float32,
        )
    for i in range(1, 8):
        waits.append(wires.send(d_buf.at[lax.rem(me + i, 8)], dp_ref.at[me], z_at[i]))
    locals_.append(wires.local(d_buf.at[me], dp_ref.at[me]))

    for ring in rings:
        ring.first()
    for ring in rings:
        ring.second()
    for step in range(4):
        for ring in rings:
            ring.third(step)
    for step in range(4):
        for ring in rings:
            ring.fourth(step)
    for copy in waits:
        copy.wait_recv()
    for copy in locals_:
        copy.wait()
    wires.finish_sends()


def collect_kernel(
    dq_ref, dk_ref, dv_ref,
    gq_ref, gk_ref, gv_ref,
    mine_k, mine_v, sib_k, sib_v, far_k, far_v, near_k, near_v, end_k, end_v,
    send_sem, recv_sem, local_sem,
):
    me = lax.axis_index("kv")
    x, y, c, at = place()
    z_at = [{"kv": lax.rem(me + i, 8)} for i in range(8)]
    greet(z_at[1:] + [at(1, 0), at(-1, 0), at(0, 1), at(0, -1), at(0, 0, 1)])
    wires = Wires(send_sem, recv_sem, local_sem)
    f32, bf16 = jnp.float32, jnp.bfloat16
    waits = []
    lo, hi = pl.ds(0, 256), pl.ds(256, 256)
    order = (
        (2, 2), (-1, 2), (1, 2), (0, 2),
        (-1, 1), (2, -1), (1, -1),
        (2, 1), (-1, -1), (1, 1), (0, -1), (0, 1),
        (2, 0), (1, 0), (-1, 0), (0, 0),
    )

    class Ring:
        def __init__(self, src, mine, sib, far, near, end, x_first):
            self.src, self.mine, self.sib = src, mine, sib
            self.far, self.near, self.end, self.x_first = far, near, end, x_first
            self.swaps, self.fars, self.nears = {}, {}, {}

        def dev(self, da, db):
            return at(da, db) if self.x_first else at(db, da)

        def cell(self, ref, da, db):
            dx, dy = (da, db) if self.x_first else (db, da)
            return ref.at[wrap4(x + dx), wrap4(y + dy)]

        def swap(self, da, db):
            self.swaps[da, db] = wires.send(
                self.cell(self.src, da, db).at[1 - c], self.cell(self.sib, da, db), at(0, 0, 1)
            )

        def pair(self, da, db):
            self.swaps[da, db].wait_recv()
            here = self.cell(self.src, da, db).at[c]
            return here[...].astype(f32) + self.cell(self.sib, da, db)[...].astype(f32)

        def send(self, piece, da, db, dst, device):
            m = self.cell(self.mine, da, db)
            m[...] = piece.astype(bf16)
            return wires.send(m, dst, device)

        def to_far(self, da):
            up = da > 0
            side = 0 if up else 1
            i = (2, 1).index(da) if up else (-1, 0).index(da)
            self.fars[da] = self.send(
                self.pair(da, 2), da, 2, self.far.at[side, i], self.dev(0, 1 if up else -1)
            )

        def to_near(self, da, db):
            piece = self.pair(da, db)
            side = 0 if db == 1 else 1
            if (da > 0) == (db == 1):
                i = (2, 1).index(da) if da > 0 else (-1, 0).index(da)
                self.fars[da].wait_recv()
                piece = piece + self.far[side, i].astype(f32)
            self.nears[da, db] = self.send(
                piece, da, db, self.near.at[side, da % 4], self.dev(0, db)
            )

        def total(self, da):
            piece = self.pair(da, 0)
            self.nears[da, -1].wait_recv()
            piece = piece + self.near[1, da % 4].astype(f32)
            self.nears[da, 1].wait_recv()
            return piece + self.near[0, da % 4].astype(f32)

        def turn(self):
            m = self.cell(self.mine, 2, 0)
            m[...] = self.total(2).astype(bf16)
            self.end_far_p = wires.send(m.at[lo], self.end.at[0, lo], self.dev(1, 0))
            self.end_far_m = wires.send(m.at[hi], self.end.at[0, hi], self.dev(-1, 0))

        def side(self, da):
            m = self.cell(self.mine, da, 0)
            piece = self.total(da)
            if da == 1:
                m[hi] = piece[256:].astype(bf16)
                self.end_far_p.wait_recv()
                m[lo] = (piece[:256] + self.end[0, lo].astype(f32)).astype(bf16)
                self.end_p = wires.send(m, self.end.at[1], self.dev(1, 0))
            else:
                m[lo] = piece[:256].astype(bf16)
                self.end_far_m.wait_recv()
                m[hi] = (piece[256:] + self.end[0, hi].astype(f32)).astype(bf16)
                self.end_m = wires.send(m, self.end.at[2], self.dev(-1, 0))

        def last(self, out, scale):
            t = self.total(0)
            self.end_p.wait_recv()
            t = t + self.end[1].astype(f32)
            self.end_m.wait_recv()
            t = t + self.end[2].astype(f32)
            out[...] = (t * scale).astype(bf16)

    rings = (
        Ring(dk_ref, mine_k, sib_k, far_k, near_k, end_k, True),
        Ring(dv_ref, mine_v, sib_v, far_v, near_v, end_v, False),
    )
    for da, db in order:
        for ring in rings:
            ring.swap(da, db)

    def rows(i):
        return pl.ds(pl.multiple_of(lax.rem(me + i, 8) * 32, 32), 32)

    cols = pl.ds(pl.multiple_of(me * 1024, 1024), 1024)
    for i in (4, 3, 5, 2, 6, 1, 7):
        waits.append(wires.send(dq_ref.at[rows(i), :], gq_ref.at[:, cols], z_at[i]))
    own = wires.local(dq_ref.at[rows(0), :], gq_ref.at[:, cols])
    for da, db in order[:12]:
        for ring in rings:
            if db == 2:
                ring.to_far(da)
            else:
                ring.to_near(da, db)
    for ring in rings:
        ring.turn()
    for da in (1, -1):
        for ring in rings:
            ring.side(da)
    rings[0].last(gk_ref, 1.0 / math.sqrt(128.0))
    rings[1].last(gv_ref, 1.0)
    for copy in waits:
        copy.wait_recv()
    own.wait()
    wires.finish_sends()


ANY = pl.BlockSpec(memory_space=pl.ANY)
HBM = pl.BlockSpec(memory_space=pltpu.HBM)
VM = pl.BlockSpec(memory_space=pltpu.VMEM)
SM = pl.BlockSpec(memory_space=pltpu.SMEM)
DMA = pltpu.SemaphoreType.DMA


def spread(q, o, g, k, v):
    bf16 = jnp.bfloat16
    rows = jax.ShapeDtypeStruct((256, 1024), bf16)
    cache = jax.ShapeDtypeStruct((4, 4, 2, 512, 128), bf16)
    return pl.pallas_call(
        spread_kernel,
        out_shape=(rows, rows, jax.ShapeDtypeStruct((8, 8, 128), jnp.float32), cache, cache),
        in_specs=[HBM] * 5,
        out_specs=(ANY,) * 5,
        scratch_shapes=[
            pltpu.VMEM((32, 8192), bf16),
            pltpu.VMEM((32, 8192), bf16),
            pltpu.VMEM((8, 8, 128), jnp.float32),
            DMA((96,)),
            DMA((96,)),
            DMA((8,)),
        ],
        compiler_params=pltpu.CompilerParams(
            collective_id=0, has_side_effects=True, vmem_limit_bytes=4 * 2**20
        ),
    )(q, o, g, k, v)


def collect(dq, dk, dv):
    bf16 = jnp.bfloat16
    out = jax.ShapeDtypeStruct((512, 128), bf16)
    return pl.pallas_call(
        collect_kernel,
        out_shape=(jax.ShapeDtypeStruct((32, 8192), bf16), out, out),
        in_specs=[ANY, VM, VM],
        out_specs=(ANY, VM, VM),
        scratch_shapes=[
            pltpu.VMEM((4, 4, 512, 128), bf16),
            pltpu.VMEM((4, 4, 512, 128), bf16),
            pltpu.VMEM((4, 4, 512, 128), bf16),
            pltpu.VMEM((4, 4, 512, 128), bf16),
            pltpu.VMEM((2, 2, 512, 128), bf16),
            pltpu.VMEM((2, 2, 512, 128), bf16),
            pltpu.VMEM((2, 4, 512, 128), bf16),
            pltpu.VMEM((2, 4, 512, 128), bf16),
            pltpu.VMEM((3, 512, 128), bf16),
            pltpu.VMEM((3, 512, 128), bf16),
            DMA((72,)),
            DMA((72,)),
            DMA((1,)),
        ],
        compiler_params=pltpu.CompilerParams(
            collective_id=1, has_side_effects=True, vmem_limit_bytes=20 * 2**20
        ),
    )(dq, dk, dv)


def on_device(
    query_rows, attn_out, grad_out, logsumexp, key_cache, value_cache, block_lists, block_counts
):
    def stay(a):
        return pltpu.with_memory_space_constraint(a, pltpu.HBM)

    q, g, dp, kf, vf = spread(
        stay(query_rows), stay(attn_out), stay(grad_out), stay(key_cache), stay(value_cache)
    )
    blocks = (128, 128, 128)
    dq, dk, dv = grads(
        stay(block_lists),
        stay(block_counts.T),
        q,
        g,
        stay(logsumexp),
        dp,
        kf.reshape(blocks),
        vf.reshape(blocks),
    )
    gq, gk, gv = collect(dq, dk.reshape(kf.shape), dv.reshape(vf.shape))
    return gq, gk[None], gv[None]


def solution(mesh):
    placed = (
        P(("seq", "kv"), None),
        P(("seq", "kv"), None),
        P(("seq", "kv"), None),
        P("kv", "seq"),
        P("kv", "seq", None),
        P("kv", "seq", None),
        P("kv", "seq", None),
        P("kv", "seq"),
    )
    return jax.shard_map(
        on_device,
        mesh=mesh,
        in_specs=placed,
        out_specs=(P(("seq", "kv"), None), P("kv", "seq", None), P("kv", "seq", None)),
        check_vma=False,
    )
```

time: 130 us -> 89.8 us (0.69)
  the two profiles are of different devices: /device:TPU:2 before, /device:TPU:1 now
where the time goes in v2:
time: 89.8 us; the launch traced here: 89.7 us
  Pallas kernels  86.9 us (97%)
  local copies, waits for them, and re-layouts  2.11 us (2%)
    pallas_call x1, Pallas kernels, spread(): pl.pallas_call(spread_kernel, out_shape=(rows, rows, jax.ShapeDtypeStruct...  39.8 us
    pallas_call x1, Pallas kernels, collect(): pl.pallas_call(collect_kernel, out_shape=(jax.ShapeDtypeStruct((32, 8192)...  29.5 us
    pallas_call x1, Pallas kernels, grads(): pl.pallas_call(grads_kernel, out_shape=(jax.ShapeDtypeStruct((256, 1024),...  17.7 us
    unnamed x3, local copies, waits for them, and re-layouts  2.11 us

profile of v2, /device:TPU:1, one launch (start us, length us, event | category | flops | bytes accessed | tf_op | source)
XLA Modules:
  0.0 89.7 jit_solution(4326830454017620151)
XLA Ops:
  0.6 39.8 %shard_map.103 = (bf16[256,1024]{1,0:T(8,128)(2,1)S(1)}, bf16[256,1024]{1,0:T(8,128)(2,1)S(1)}, f32[8,8,128]{2,1,0:T(8,128)S(1)}, bf16[4,4,2,512,128]{4,3,2,1,0:...) custom-call(bf16[32,8192]{1,0:T(8,128)(2,1)} %q_ref.1, bf16[32,8192]{1,0:T(8,128)(2,1)} %o_ref.1, bf16[32,8192]{1,0:T(8,128)(2,1)} %g_ref.1, ...), custom_call_target="tpu_custom_call" | custom-call | tf_op jit(solution)/shard_map/pallas_call | solution.py:559
  40.4 17.7 %shard_map.104 = (bf16[256,1024]{1,0:T(8,128)(2,1)S(1)}, bf16[128,128,128]{2,1,0:T(8,128)(2,1)S(1)}, bf16[128,128,128]{2,1,0:T(8,128)(2,1)S(1)}) custom-call(s32[8,2,32]{2,1,0:T(2,128)} %lists_hbm.1, s32[2,8]{1,0:T(2,128)} %bitcast.13, bf16[256,1024]{1,0:T(8,128)(2,1)S(1)} %get-tuple-element.14.q_ref, bf16[256,1024]{1,0:T(8,128)(2,1)S(1)} %get-tuple-element.15.do_ref, ...), custom_call_target="tpu_custom_call" | custom-call | tf_op jit(solution)/shard_map/pallas_call | solution.py:166
  58.1 29.5 %shard_map.105 = (bf16[32,8192]{1,0:T(8,128)(2,1)S(1)}, bf16[512,128]{1,0:T(8,128)(2,1)S(1)}, bf16[512,128]{1,0:T(8,128)(2,1)S(1)}) custom-call(bf16[256,1024]{1,0:T(8,128)(2,1)S(1)} %get-tuple-element.19.dq_ref, bf16[4,4,2,512,128]{4,3,2,1,0:T(8,128)(2,1)S(1)} %bitcast.9, bf16[4,4,2,512,128]{4,3,2,1,0:T(8,128)(2,1)S(1)} %bitcast.10), custom_call_target="tpu_custom_call" | custom-call | tf_op jit(solution)/shard_map/pallas_call | solution.py:581
  87.6 0.8 copy.14
  88.4 0.7 copy.15
  89.0 0.7 copy.16

commit v3 on v2

--- a/solution.py
+++ b/solution.py
@@ -49,11 +49,8 @@
 
         return lax.fori_loop(0, (counts[lax.rem(r, 2), r // 2] + (G - 1)) // G, put, n)
 
-    for i in range(UNROLL):
-        row_of[i] = 0
-        at_of[i] = 32
-    total = lax.fori_loop(0, 16, list_row, UNROLL)
-    for i in range(3 * UNROLL):
+    total = lax.fori_loop(0, 16, list_row, 0)
+    for i in range(2 * UNROLL):
         row_of[total + i] = 0
         at_of[total + i] = 32
 
@@ -126,23 +123,30 @@
         )
         return r, blocks, out, dq
 
-    def half(e, write, read):
+    def score_step(k, write):
         for u in range(UNROLL):
-            score(e + UNROLL + u, write.at[u])
-        for r, blocks, out, dq in [terms(e + u, read.at[u]) for u in range(UNROLL)]:
+            score(k * UNROLL + u, write.at[u])
+
+    def step(k, write, read):
+        score_step(k + 1, write)
+        for r, blocks, out, dq in [terms(k * UNROLL + u, read.at[u]) for u in range(UNROLL)]:
             dqa[r] += dq
             for i in range(G):
                 acc[blocks[i]] += out[i * BLK : (i + 1) * BLK]
 
-    def some_groups(m, _):
-        half(2 * m * UNROLL, slot_a, slot_b)
-        half((2 * m + 1) * UNROLL, slot_b, slot_a)
+    steps = (total + UNROLL - 1) // UNROLL
+
+    def two_steps(m, _):
+        step(2 * m, slot_b, slot_a)
+
+        @pl.when(2 * m + 1 < steps)
+        def _():
+            step(2 * m + 1, slot_a, slot_b)
+
         return 0
 
-    for u in range(UNROLL):
-        slot_b[u] = jnp.zeros((G * BLK, 2 * BLK), f32)
-    halves_needed = (total - UNROLL + UNROLL - 1) // UNROLL + 1
-    lax.fori_loop(0, (halves_needed + 1) // 2, some_groups, 0)
+    score_step(0, slot_a)
+    lax.fori_loop(0, (steps + 1) // 2, two_steps, 0)
 
     def finish_block(i, _):
         a = acc[i]
@@ -244,6 +248,9 @@
     return x, y, c, at
 
 
+SLOTS = ((1, 4), (1, 3), (1, 2), (2, 4), (2, 3), (3, 4))
+
+
 def wrap4(i):
     return lax.rem(i + 4, 4)
 
@@ -251,12 +258,12 @@
 def spread_kernel(
     q_ref, o_ref, g_ref, k_ref, v_ref,
     qo_ref, go_ref, dp_ref, kf_ref, vf_ref,
-    o_buf, g_buf, d_buf, send_sem, recv_sem, local_sem,
+    o_buf, g_buf, d_buf, relay, d_relay, send_sem, recv_sem, local_sem,
 ):
     me = lax.axis_index("kv")
     x, y, c, at = place()
-    z_at = [{"kv": lax.rem(me + i, 8)} for i in range(8)]
-    greet(z_at[1:] + [at(1, 0), at(-1, 0), at(0, 1), at(0, -1), at(0, 0, 1)])
+    z_at = {sign: {"kv": lax.rem(me + 8 + sign, 8)} for sign in (1, -1)}
+    greet([z_at[1], z_at[-1], at(1, 0), at(-1, 0), at(0, 1), at(0, -1), at(0, 0, 1)])
     wires = Wires(send_sem, recv_sem, local_sem)
     locals_ = []
     waits = []
@@ -362,9 +369,45 @@
     def columns(i):
         return pl.ds(pl.multiple_of(lax.rem(me + i, 8) * 1024, 1024), 1024)
 
-    for i in (1, 7, 2, 6, 3, 5, 4):
-        for src, dst in ((q_ref, qo_ref), (g_ref, go_ref)):
-            waits.append(wires.send(src.at[:, columns(i)], dst.at[rows, :], z_at[i]))
+    moved = {}
+
+    def z_hop(hop, far):
+        for a, (src, dst) in enumerate(((q_ref, qo_ref), (g_ref, go_ref))):
+            for side, sign in enumerate((1, -1)):
+                first, count = (16 * side, 16) if far == 4 else (0, 32)
+                if hop == 1:
+                    part = src.at[pl.ds(first, count), columns(8 + sign * far)]
+                else:
+                    moved[a, side, hop - 1, far].wait_recv()
+                    part = relay.at[a, side, SLOTS.index((hop - 1, far)), pl.ds(0, count)]
+                if hop == far:
+                    start = lax.rem(me + 8 - sign * (hop - 1), 8) * 32 + first
+                    there = dst.at[pl.ds(pl.multiple_of(start, 16), count), :]
+                else:
+                    there = relay.at[a, side, SLOTS.index((hop, far)), pl.ds(0, count)]
+                copy = wires.send(part, there, z_at[sign])
+                moved[a, side, hop, far] = copy
+                if hop == far:
+                    waits.append(copy)
+
+    def delta_hop(hop, far):
+        for side, sign in enumerate((1, -1) if far < 4 else (1,)):
+            if hop == 1:
+                part = d_buf.at[lax.rem(me + 8 + sign * far, 8)]
+            else:
+                moved[2, side, hop - 1, far].wait_recv()
+                part = d_relay.at[side, SLOTS.index((hop - 1, far))]
+            if hop == far:
+                there = dp_ref.at[lax.rem(me + 8 - sign * (hop - 1), 8)]
+            else:
+                there = d_relay.at[side, SLOTS.index((hop, far))]
+            copy = wires.send(part, there, z_at[sign])
+            moved[2, side, hop, far] = copy
+            if hop == far:
+                waits.append(copy)
+
+    for far in (4, 3):
+        z_hop(1, far)
     for src, dst in ((q_ref, qo_ref), (g_ref, go_ref)):
         locals_.append(wires.local(src.at[:, columns(0)], dst.at[rows, :]))
     for ring in rings:
@@ -387,17 +430,30 @@
             precision=lax.Precision.HIGHEST,
             preferred_element_type=jnp.float32,
         )
-    for i in range(1, 8):
-        waits.append(wires.send(d_buf.at[lax.rem(me + i, 8)], dp_ref.at[me], z_at[i]))
+    for far in (4, 3, 2, 1):
+        delta_hop(1, far)
+    for far in (2, 1):
+        z_hop(1, far)
     locals_.append(wires.local(d_buf.at[me], dp_ref.at[me]))
 
     for ring in rings:
         ring.first()
+    for far in (4, 3, 2):
+        z_hop(2, far)
+        delta_hop(2, far)
     for ring in rings:
         ring.second()
-    for step in range(4):
+    for step in range(2):
         for ring in rings:
             ring.third(step)
+    for far in (4, 3):
+        z_hop(3, far)
+        delta_hop(3, far)
+    for step in range(2, 4):
+        for ring in rings:
+            ring.third(step)
+    z_hop(4, 4)
+    delta_hop(4, 4)
     for step in range(4):
         for ring in rings:
             ring.fourth(step)
@@ -411,13 +467,13 @@
 def collect_kernel(
     dq_ref, dk_ref, dv_ref,
     gq_ref, gk_ref, gv_ref,
-    mine_k, mine_v, sib_k, sib_v, far_k, far_v, near_k, near_v, end_k, end_v,
+    mine_k, mine_v, sib_k, sib_v, far_k, far_v, near_k, near_v, end_k, end_v, relay,
     send_sem, recv_sem, local_sem,
 ):
     me = lax.axis_index("kv")
     x, y, c, at = place()
-    z_at = [{"kv": lax.rem(me + i, 8)} for i in range(8)]
-    greet(z_at[1:] + [at(1, 0), at(-1, 0), at(0, 1), at(0, -1), at(0, 0, 1)])
+    z_at = {sign: {"kv": lax.rem(me + 8 + sign, 8)} for sign in (1, -1)}
+    greet([z_at[1], z_at[-1], at(1, 0), at(-1, 0), at(0, 1), at(0, -1), at(0, 0, 1)])
     wires = Wires(send_sem, recv_sem, local_sem)
     f32, bf16 = jnp.float32, jnp.bfloat16
     waits = []
@@ -519,21 +575,47 @@
         for ring in rings:
             ring.swap(da, db)
 
-    def rows(i):
-        return pl.ds(pl.multiple_of(lax.rem(me + i, 8) * 32, 32), 32)
-
-    cols = pl.ds(pl.multiple_of(me * 1024, 1024), 1024)
-    for i in (4, 3, 5, 2, 6, 1, 7):
-        waits.append(wires.send(dq_ref.at[rows(i), :], gq_ref.at[:, cols], z_at[i]))
-    own = wires.local(dq_ref.at[rows(0), :], gq_ref.at[:, cols])
-    for da, db in order[:12]:
+    def columns(i):
+        return pl.ds(pl.multiple_of(lax.rem(me + 8 + i, 8) * 1024, 1024), 1024)
+
+    moved = {}
+
+    def z_hop(hop, far):
+        for side, sign in enumerate((1, -1)):
+            first, count = (16 * side, 16) if far == 4 else (0, 32)
+            if hop == 1:
+                start = lax.rem(me + 8 + sign * far, 8) * 32 + first
+                part = dq_ref.at[pl.ds(pl.multiple_of(start, 16), count), :]
+            else:
+                moved[side, hop - 1, far].wait_recv()
+                part = relay.at[side, SLOTS.index((hop - 1, far)), pl.ds(0, count)]
+            if hop == far:
+                there = gq_ref.at[pl.ds(first, count), columns(-sign * (hop - 1))]
+            else:
+                there = relay.at[side, SLOTS.index((hop, far)), pl.ds(0, count)]
+            copy = wires.send(part, there, z_at[sign])
+            moved[side, hop, far] = copy
+            if hop == far:
+                waits.append(copy)
+
+    for far in (4, 3, 2, 1):
+        z_hop(1, far)
+    mine = pl.ds(pl.multiple_of(me * 32, 32), 32)
+    own = wires.local(dq_ref.at[mine, :], gq_ref.at[:, columns(0)])
+    for step, (da, db) in enumerate(order[:12]):
         for ring in rings:
             if db == 2:
                 ring.to_far(da)
             else:
                 ring.to_near(da, db)
+        if step == 7:
+            for far in (4, 3, 2):
+                z_hop(2, far)
+    for far in (4, 3):
+        z_hop(3, far)
     for ring in rings:
         ring.turn()
+    z_hop(4, 4)
     for da in (1, -1):
         for ring in rings:
             ring.side(da)
@@ -565,8 +647,10 @@
             pltpu.VMEM((32, 8192), bf16),
             pltpu.VMEM((32, 8192), bf16),
             pltpu.VMEM((8, 8, 128), jnp.float32),
-            DMA((96,)),
-            DMA((96,)),
+            pltpu.VMEM((2, 2, 6, 32, 1024), bf16),
+            pltpu.VMEM((2, 6, 8, 128), jnp.float32),
+            DMA((144,)),
+            DMA((144,)),
             DMA((8,)),
         ],
         compiler_params=pltpu.CompilerParams(
@@ -594,8 +678,9 @@
             pltpu.VMEM((2, 4, 512, 128), bf16),
             pltpu.VMEM((3, 512, 128), bf16),
             pltpu.VMEM((3, 512, 128), bf16),
-            DMA((72,)),
-            DMA((72,)),
+            pltpu.VMEM((2, 6, 32, 1024), bf16),
+            DMA((96,)),
+            DMA((96,)),
             DMA((1,)),
         ],
         compiler_params=pltpu.CompilerParams(

time: 89.8 us -> 86.6 us (0.964)
  Pallas kernels: 86.9 us -> 83.8 us
    pallas_call x1, Pallas kernels: 17.7 us -> 12.2 us  [grads(): pl.pallas_call(grads_kernel, out_shape=(jax.ShapeDtypeStruct((256, 1024),...]
    pallas_call x1, Pallas kernels: 29.5 us -> 32.2 us  [collect(): pl.pallas_call(collect_kernel, out_shape=(jax.ShapeDtypeStruct((32, 8192)...]
where the time goes in v3:
time: 86.6 us; the launch traced here: 86.5 us
  Pallas kernels  83.8 us (97%)
  local copies, waits for them, and re-layouts  2.11 us (2%)
    pallas_call x1, Pallas kernels, spread(): pl.pallas_call(spread_kernel, out_shape=(rows, rows, jax.ShapeDtypeStruct...  39.3 us
    pallas_call x1, Pallas kernels, collect(): pl.pallas_call(collect_kernel, out_shape=(jax.ShapeDtypeStruct((32, 8192)...  32.2 us
    pallas_call x1, Pallas kernels, grads(): pl.pallas_call(grads_kernel, out_shape=(jax.ShapeDtypeStruct((256, 1024),...  12.2 us
    unnamed x3, local copies, waits for them, and re-layouts  2.11 us

profile of v3, /device:TPU:1, one launch (start us, length us, event | category | flops | bytes accessed | tf_op | source)
XLA Modules:
  0.0 86.5 jit_solution(12744936979416584413)
XLA Ops:
  0.6 39.3 %shard_map.103 = (bf16[256,1024]{1,0:T(8,128)(2,1)S(1)}, bf16[256,1024]{1,0:T(8,128)(2,1)S(1)}, f32[8,8,128]{2,1,0:T(8,128)S(1)}, bf16[4,4,2,512,128]{4,3,2,1,0:...) custom-call(bf16[32,8192]{1,0:T(8,128)(2,1)} %q_ref.1, bf16[32,8192]{1,0:T(8,128)(2,1)} %o_ref.1, bf16[32,8192]{1,0:T(8,128)(2,1)} %g_ref.1, ...), custom_call_target="tpu_custom_call" | custom-call | tf_op jit(solution)/shard_map/pallas_call | solution.py:641
  40.0 12.2 %shard_map.104 = (bf16[256,1024]{1,0:T(8,128)(2,1)S(1)}, bf16[128,128,128]{2,1,0:T(8,128)(2,1)S(1)}, bf16[128,128,128]{2,1,0:T(8,128)(2,1)S(1)}) custom-call(s32[8,2,32]{2,1,0:T(2,128)} %lists_hbm.1, s32[2,8]{1,0:T(2,128)} %bitcast.13, bf16[256,1024]{1,0:T(8,128)(2,1)S(1)} %get-tuple-element.14.q_ref, bf16[256,1024]{1,0:T(8,128)(2,1)S(1)} %get-tuple-element.15.do_ref, ...), custom_call_target="tpu_custom_call" | custom-call | tf_op jit(solution)/shard_map/pallas_call | solution.py:170
  52.2 32.2 %shard_map.105 = (bf16[32,8192]{1,0:T(8,128)(2,1)S(1)}, bf16[512,128]{1,0:T(8,128)(2,1)S(1)}, bf16[512,128]{1,0:T(8,128)(2,1)S(1)}) custom-call(bf16[256,1024]{1,0:T(8,128)(2,1)S(1)} %get-tuple-element.19.dq_ref, bf16[4,4,2,512,128]{4,3,2,1,0:T(8,128)(2,1)S(1)} %bitcast.9, bf16[4,4,2,512,128]{4,3,2,1,0:T(8,128)(2,1)S(1)} %bitcast.10), custom_call_target="tpu_custom_call" | custom-call | tf_op jit(solution)/shard_map/pallas_call | solution.py:665
  84.4 0.8 copy.14
  85.2 0.7 copy.15
  85.9 0.7 copy.16

commit v4 on v3

--- a/solution.py
+++ b/solution.py
@@ -38,18 +38,38 @@
 
     lax.fori_loop(0, 128, zero, 0, unroll=4)
 
+    blank = jnp.zeros((BLK, BLK), bf16)
+
+    def place_of(r):
+        h, qb = r // 2, lax.rem(r, 2)
+        return (
+            pl.ds(pl.multiple_of(qb * BLK, BLK), BLK),
+            pl.ds(pl.multiple_of(h * BLK, BLK), BLK),
+        )
+
+    def diagonal(a, b):
+        return jnp.concatenate(
+            [jnp.concatenate([a, blank], axis=1), jnp.concatenate([blank, b], axis=1)], axis=0
+        )
+
+    def prepare(r, _):
+        q = q_ref[place_of(r)]
+        d = do_ref[place_of(r)]
+        w1[r] = diagonal(q.T, d.T)
+        w2[r] = diagonal(q, d)
+        dqa[r] = jnp.zeros((BLK, BLK), f32)
+        return 0
+
+    lax.fori_loop(0, 16, prepare, 0, unroll=4)
     for copy in copies:
         copy.wait()
 
-    def list_row(r, n):
-        def put(g, n):
-            row_of[n] = r
-            at_of[n] = g * G
-            return n + 1
-
-        return lax.fori_loop(0, (counts[lax.rem(r, 2), r // 2] + (G - 1)) // G, put, n)
-
-    total = lax.fori_loop(0, 16, list_row, 0)
+    total = jnp.int32(0)
+    for r in range(16):
+        for g in range(32 // G):
+            row_of[total + g] = r
+            at_of[total + g] = g * G
+        total = total + (counts[r % 2, r // 2] + (G - 1)) // G
     for i in range(2 * UNROLL):
         row_of[total + i] = 0
         at_of[total + i] = 32
@@ -62,29 +82,6 @@
         for h in range(8):
             row_delta[2 * h + qb] = d[h : h + 1]
             row_lse[2 * h + qb] = l[h : h + 1]
-    blank = jnp.zeros((BLK, BLK), bf16)
-
-    def place_of(r):
-        h, qb = r // 2, lax.rem(r, 2)
-        return (
-            pl.ds(pl.multiple_of(qb * BLK, BLK), BLK),
-            pl.ds(pl.multiple_of(h * BLK, BLK), BLK),
-        )
-
-    def diagonal(a, b):
-        return jnp.concatenate(
-            [jnp.concatenate([a, blank], axis=1), jnp.concatenate([blank, b], axis=1)], axis=0
-        )
-
-    def prepare(r, _):
-        q = q_ref[place_of(r)]
-        d = do_ref[place_of(r)]
-        w1[r] = diagonal(q.T, d.T)
-        w2[r] = diagonal(q, d)
-        dqa[r] = jnp.zeros((BLK, BLK), f32)
-        return 0
-
-    lax.fori_loop(0, 16, prepare, 0, unroll=4)
     causal = lax.broadcasted_iota(jnp.int32, (BLK, BLK), 0) <= lax.broadcasted_iota(
         jnp.int32, (BLK, BLK), 1
     )
@@ -406,7 +403,7 @@
             if hop == far:
                 waits.append(copy)
 
-    for far in (4, 3):
+    for far in (4, 3, 2):
         z_hop(1, far)
     for src, dst in ((q_ref, qo_ref), (g_ref, go_ref)):
         locals_.append(wires.local(src.at[:, columns(0)], dst.at[rows, :]))
@@ -432,8 +429,7 @@
         )
     for far in (4, 3, 2, 1):
         delta_hop(1, far)
-    for far in (2, 1):
-        z_hop(1, far)
+    z_hop(1, 1)
     locals_.append(wires.local(d_buf.at[me], dp_ref.at[me]))
 
     for ring in rings:
@@ -454,7 +450,7 @@
             ring.third(step)
     z_hop(4, 4)
     delta_hop(4, 4)
-    for step in range(4):
+    for step in (0, 2, 1, 3):
         for ring in rings:
             ring.fourth(step)
     for copy in waits:
@@ -466,7 +462,7 @@
 
 def collect_kernel(
     dq_ref, dk_ref, dv_ref,
-    gq_ref, gk_ref, gv_ref,
+    gq_ref, gkv_ref,
     mine_k, mine_v, sib_k, sib_v, far_k, far_v, near_k, near_v, end_k, end_v, relay,
     send_sem, recv_sem, local_sem,
 ):
@@ -619,8 +615,8 @@
     for da in (1, -1):
         for ring in rings:
             ring.side(da)
-    rings[0].last(gk_ref, 1.0 / math.sqrt(128.0))
-    rings[1].last(gv_ref, 1.0)
+    rings[0].last(gkv_ref.at[0], 1.0 / math.sqrt(128.0))
+    rings[1].last(gkv_ref.at[1], 1.0)
     for copy in waits:
         copy.wait_recv()
     own.wait()
@@ -661,12 +657,12 @@
 
 def collect(dq, dk, dv):
     bf16 = jnp.bfloat16
-    out = jax.ShapeDtypeStruct((512, 128), bf16)
+    out = jax.ShapeDtypeStruct((2, 512, 128), bf16)
     return pl.pallas_call(
         collect_kernel,
-        out_shape=(jax.ShapeDtypeStruct((32, 8192), bf16), out, out),
+        out_shape=(jax.ShapeDtypeStruct((32, 8192), bf16), out),
         in_specs=[ANY, VM, VM],
-        out_specs=(ANY, VM, VM),
+        out_specs=(ANY, VM),
         scratch_shapes=[
             pltpu.VMEM((4, 4, 512, 128), bf16),
             pltpu.VMEM((4, 4, 512, 128), bf16),
@@ -709,8 +705,8 @@
         kf.reshape(blocks),
         vf.reshape(blocks),
     )
-    gq, gk, gv = collect(dq, dk.reshape(kf.shape), dv.reshape(vf.shape))
-    return gq, gk[None], gv[None]
+    gq, pair = collect(dq, dk.reshape(kf.shape), dv.reshape(vf.shape))
+    return gq, pair[:1], pair[1:]
 
 
 def solution(mesh):

time: 86.6 us -> 85.8 us (level)
    pallas_call x1, Pallas kernels: 12.2 us -> 15.3 us  [grads(): pl.pallas_call(grads_kernel, out_shape=(jax.ShapeDtypeStruct((256, 1024),...]
    pallas_call x1, Pallas kernels: 32.2 us -> 29.3 us  [collect(): pl.pallas_call(collect_kernel, out_shape=(jax.ShapeDtypeStruct((32, 8192)...]
    unnamed x3 -> x1, local copies, waits for them, and re-layouts: 2.11 us -> 0.79 us
where the time goes in v4:
time: 85.8 us; the launch traced here: 85.7 us
  Pallas kernels  83.6 us (97%)
  local copies, waits for them, and re-layouts  1.51 us (2%)
    pallas_call x1, Pallas kernels, spread(): pl.pallas_call(spread_kernel, out_shape=(rows, rows, jax.ShapeDtypeStruct...  38.9 us
    pallas_call x1, Pallas kernels, collect(): pl.pallas_call(collect_kernel, out_shape=(jax.ShapeDtypeStruct((32, 8192)...  29.3 us
    pallas_call x1, Pallas kernels, grads(): pl.pallas_call(grads_kernel, out_shape=(jax.ShapeDtypeStruct((256, 1024),...  15.3 us

profile of v4, /device:TPU:1, one launch (start us, length us, event | category | flops | bytes accessed | tf_op | source)
XLA Modules:
  0.0 85.7 jit_solution(454251747872666797)
XLA Ops:
  0.6 38.9 %shard_map.103 = (bf16[256,1024]{1,0:T(8,128)(2,1)S(1)}, bf16[256,1024]{1,0:T(8,128)(2,1)S(1)}, f32[8,8,128]{2,1,0:T(8,128)S(1)}, bf16[4,4,2,512,128]{4,3,2,1,0:...) custom-call(bf16[32,8192]{1,0:T(8,128)(2,1)} %q_ref.1, bf16[32,8192]{1,0:T(8,128)(2,1)} %o_ref.1, bf16[32,8192]{1,0:T(8,128)(2,1)} %g_ref.1, ...), custom_call_target="tpu_custom_call" | custom-call | tf_op jit(solution)/shard_map/pallas_call | solution.py:637
  39.6 15.3 %shard_map.104 = (bf16[256,1024]{1,0:T(8,128)(2,1)S(1)}, bf16[128,128,128]{2,1,0:T(8,128)(2,1)S(1)}, bf16[128,128,128]{2,1,0:T(8,128)(2,1)S(1)}) custom-call(s32[8,2,32]{2,1,0:T(2,128)} %lists_hbm.1, s32[2,8]{1,0:T(2,128)} %bitcast.9, bf16[256,1024]{1,0:T(8,128)(2,1)S(1)} %get-tuple-element.13.q_ref, bf16[256,1024]{1,0:T(8,128)(2,1)S(1)} %get-tuple-element.14.do_ref, ...), custom_call_target="tpu_custom_call" | custom-call | tf_op jit(solution)/shard_map/pallas_call | solution.py:167
  54.9 29.3 %shard_map.105 = (bf16[32,8192]{1,0:T(8,128)(2,1)S(1)}, bf16[2,512,128]{2,1,0:T(8,128)(2,1)S(1)}) custom-call(bf16[256,1024]{1,0:T(8,128)(2,1)S(1)} %get-tuple-element.18.dq_ref, bf16[4,4,2,512,128]{4,3,2,1,0:T(8,128)(2,1)S(1)} %bitcast.7, bf16[4,4,2,512,128]{4,3,2,1,0:T(8,128)(2,1)S(1)} %bitcast.8), custom_call_target="tpu_custom_call" | custom-call | tf_op jit(solution)/shard_map/pallas_call | solution.py:661
  84.2 0.7 fusion
  85.0 0.8 copy.12
